TPU v7x, 256 devices: a whole 4x4x8 slice. The times are simulated.
256 devices in a mesh: dp: 16 (over z, core), node: 4 (over x), pipe: 4 (over y).
Axes of the slice: x: 4, y: 4, z: 8, core: 2. Of those that a mesh axis runs over, the one named last changes fastest.
Arguments:
- final_hidden: bfloat16 [32768, 8192], P(('dp', 'node', 'pipe')), may hold values from -128 to 128
- value_head: bfloat16 [8192, 128], replicated, may hold values from -3 to 3
- norm_gain: bfloat16 [8192], replicated, may hold values from 0.5 to 1.5
- rewards: float32 [32768], P(('dp', 'node', 'pipe')), may hold values from -6 to 6
- old_values: float32 [32768], P(('dp', 'node', 'pipe')), may hold values from -6 to 6
- loss_mask: int32 [32768], P(('dp', 'node', 'pipe')), may hold values 0 or 1
- row_exp: int32 [256, 8192], P(('dp', 'node', 'pipe')), may hold values from -14 to -11
- gain_exp: int32 [256, 64], P(('dp', 'node', 'pipe')), may hold values from -16 to -7
- first_w: float32 [8192, 128], P(('dp', 'node', 'pipe')), may hold values from -4 to 4
- second_w: float32 [8192, 128], P(('dp', 'node', 'pipe')), may hold values from 0.01 to 1
- first_g: float32 [8192], P(('dp', 'node', 'pipe')), may hold values from -4 to 4
- second_g: float32 [8192], P(('dp', 'node', 'pipe')), may hold values from 0.01 to 1
Outputs:
- new_weight: bfloat16 [8192, 128], P(('dp', 'node'))
- new_gain: bfloat16 [8192], P(('dp', 'node'))
- first_w_new: float32 [8192, 128], P(('dp', 'node', 'pipe'))
- second_w_new: float32 [8192, 128], P(('dp', 'node', 'pipe'))
- first_g_new: float32 [8192], P(('dp', 'node', 'pipe'))
- second_g_new: float32 [8192], P(('dp', 'node', 'pipe'))
All inputs are finite; a program needn't handle non-finite values. No bound on the sum of `loss_mask` on one device may be relied on, other than what follows from the above.
Results may differ from a plain program's by a relative error of at most 0.0055.
Values may be sent and summed in bfloat16 or wider, within the bound.
No kernel may reach another device: no remote copies, remote signals or barrier semaphores. Data moves between devices by JAX's collectives and lax.ppermute only.
A program may use at most 64 MiB of HBM per device.

v0:
```python
import math

import jax
import jax.numpy as jnp
from jax import lax
from jax.sharding import PartitionSpec as P

BINS = 128
GBLK = 128
SEQ = 32


LOGIT_SCALE = 0.0625
RETURN_LOW = -4.0
RETURN_HIGH = 4.0
TRACE_DECAY = 0.95
SAT_LIMIT = 448.0
LEARN_RATE = 0.02
FIRST_CORR = 0.19
SECOND_CORR = 0.0975
EPSILON = 1e-08
NORM_EPSILON = 1e-06


def gauss_targets(returns):
    width = (RETURN_HIGH - RETURN_LOW) / BINS
    spread = 0.75 * width
    bin_edges = RETURN_LOW + width * jnp.arange(BINS + 1).astype(jnp.float32)
    clamped = jnp.clip(returns, RETURN_LOW, RETURN_HIGH)
    cum_mass = 0.5 * (
        1.0
        + jax.scipy.special.erf((bin_edges[None, :] - clamped[:, None]) / (spread * math.sqrt(2.0)))
    )
    bin_mass = cum_mass[:, 1:] - cum_mass[:, :-1]
    return bin_mass / (cum_mass[:, -1:] - cum_mass[:, :1])


def gae_returns(rewards, old_values):
    reward_rows = rewards.reshape(-1, SEQ)
    value_rows = old_values.reshape(-1, SEQ)
    following = jnp.concatenate(
        [value_rows[:, 1:], jnp.zeros((value_rows.shape[0], 1), jnp.float32)], axis=1
    )
    td_error = reward_rows + following - value_rows
    row_pos = lax.broadcasted_iota(jnp.int32, (SEQ, SEQ), 0)
    col_pos = lax.broadcasted_iota(jnp.int32, (SEQ, SEQ), 1)
    offset = jnp.maximum(row_pos - col_pos, 0).astype(jnp.float32)
    kernel = jnp.where(row_pos >= col_pos, jnp.power(TRACE_DECAY, offset), 0.0)
    traced = jnp.dot(td_error, kernel, precision=lax.Precision.HIGHEST)
    return (traced + value_rows).reshape(-1)


def local_terms(hidden, gain, head, targets, mask, row_scale_exp, block_scale_exp):
    hidden_f = hidden.astype(jnp.float32)
    inv_rms = lax.rsqrt(jnp.mean(hidden_f * hidden_f, axis=1, keepdims=True) + NORM_EPSILON)
    normed = hidden_f * inv_rms
    scaled = (normed * gain.astype(jnp.float32)).astype(jnp.bfloat16)
    logits = LOGIT_SCALE * jnp.dot(scaled, head, preferred_element_type=jnp.float32)
    shifted = jnp.exp(logits - jnp.max(logits, axis=1, keepdims=True))
    probs_out = shifted / jnp.sum(shifted, axis=1, keepdims=True)
    errors = (LOGIT_SCALE * mask.astype(jnp.float32)[:, None] * (probs_out - targets)).astype(
        jnp.bfloat16
    )
    weight_part = lax.dot_general(
        scaled, errors, (((0,), (0,)), ((), ())), preferred_element_type=jnp.float32
    )
    back_prop = lax.dot_general(
        errors, head, (((1,), (1,)), ((), ())), preferred_element_type=jnp.float32
    )
    gain_part = jnp.sum(back_prop * normed, axis=0)
    row_limit = SAT_LIMIT * jnp.exp2(row_scale_exp.astype(jnp.float32))
    block_limit = SAT_LIMIT * jnp.repeat(jnp.exp2(block_scale_exp.astype(jnp.float32)), GBLK)
    weight_q = jnp.clip(weight_part, -row_limit[:, None], row_limit[:, None]).astype(jnp.bfloat16)
    gain_q = jnp.clip(gain_part, -block_limit, block_limit).astype(jnp.bfloat16)
    weight_q, gain_q = lax.optimization_barrier((weight_q, gain_q))
    return (weight_q.astype(jnp.float32), gain_q.astype(jnp.float32))


def adam_update(param, grad, first, second):
    first_new = 0.9 * first + 0.1 * grad
    second_new = 0.95 * second + 0.05 * grad * grad
    update = first_new / FIRST_CORR / (jnp.sqrt(second_new / SECOND_CORR) + EPSILON)
    return (
        (param.astype(jnp.float32) - LEARN_RATE * update).astype(jnp.bfloat16),
        first_new,
        second_new,
    )


def shards(
    final_hidden,
    value_head,
    norm_gain,
    rewards,
    old_values,
    loss_mask,
    row_exp,
    gain_exp,
    first_w,
    second_w,
    first_g,
    second_g,
):
    targets = gauss_targets(gae_returns(rewards, old_values))
    weight_q, gain_q = local_terms(
        final_hidden, norm_gain, value_head, targets, loss_mask, row_exp[0], gain_exp[0]
    )
    size_dp = lax.axis_size("dp")
    size_node = lax.axis_size("node")
    size_pipe = lax.axis_size("pipe")
    row_count = first_g.shape[0]
    bin_count = value_head.shape[1]
    total_groups = size_dp * size_node * size_pipe
    summed = (
        weight_q.reshape(total_groups, row_count, bin_count),
        gain_q.reshape(total_groups, row_count),
    )
    summed = (
        lax.psum_scatter(summed[0], ("dp", "node", "pipe"), scatter_dimension=0, tiled=True),
        lax.psum_scatter(summed[1], ("dp", "node", "pipe"), scatter_dimension=0, tiled=True),
    )
    grad_w = summed[0].reshape(row_count, bin_count)
    grad_g = summed[1].reshape(row_count)
    position = (
        lax.axis_index("dp") * size_node + lax.axis_index("node")
    ) * size_pipe + lax.axis_index("pipe")
    own_weight = lax.dynamic_slice_in_dim(value_head, position * row_count, row_count, 0)
    own_gain = lax.dynamic_slice_in_dim(norm_gain, position * row_count, row_count, 0)
    shard_weight, first_w_new, second_w_new = adam_update(own_weight, grad_w, first_w, second_w)
    shard_gain, first_g_new, second_g_new = adam_update(own_gain, grad_g, first_g, second_g)
    new_weight, new_gain = (
        lax.all_gather(shard_weight, "pipe", axis=0, tiled=True),
        lax.all_gather(shard_gain, "pipe", axis=0, tiled=True),
    )
    return (new_weight, new_gain, first_w_new, second_w_new, first_g_new, second_g_new)


def solution(mesh):
    return jax.shard_map(
        shards,
        mesh=mesh,
        in_specs=(
            P(("dp", "node", "pipe"), None),
            P(),
            P(),
            P(("dp", "node", "pipe")),
            P(("dp", "node", "pipe")),
            P(("dp", "node", "pipe")),
            P(("dp", "node", "pipe"), None),
            P(("dp", "node", "pipe"), None),
            P(("dp", "node", "pipe"), None),
            P(("dp", "node", "pipe"), None),
            P(("dp", "node", "pipe")),
            P(("dp", "node", "pipe")),
        ),
        out_specs=(
            P(("dp", "node"), None),
            P(("dp", "node")),
            P(("dp", "node", "pipe"), None),
            P(("dp", "node", "pipe"), None),
            P(("dp", "node", "pipe")),
            P(("dp", "node", "pipe")),
        ),
        check_vma=False,
    )
```

profile of v0, /device:TPU:2, one launch (start us, length us, event | category | flops | bytes accessed | tf_op | source)
XLA Modules:
  0.0 1315.1 jit_solution(1207114871956669743)
XLA Ops:
  7.2 0.0 copy-start
  7.2 0.0 reduce-scatter.2.cloned.1.call-start
  7.2 0.8 convert_multiply_fusion.2
  8.0 0.7 multiply_bitcast_fusion
  8.7 2.1 fusion.4
  10.8 0.7 reshape.93
  11.5 0.1 slice.15
  11.6 0.7 reshape.92
  12.3 0.1 fusion.6
  12.5 0.1 min.29
  12.6 0.0 copy-start.5
  12.6 0.9 convert_element_type.63
  13.5 0.8 exponential_multiply_fusion
  14.3 0.1 add_multiply_fusion
  14.4 3.3 fusion.37
  17.8 0.0 copy-done
  17.8 0.0 copy-done.5
  17.8 1.0 fusion.5
  18.9 3.4 fusion.1
  22.2 0.1 fusion.15
  22.3 0.0 copy-start.6
  22.3 0.0 copy-start.3
  22.3 0.0 copy-start.4
  22.3 0.0 copy-start.1
  22.4 0.0 copy-start.2
  22.4 2.5 convert.2
  24.9 0.0 reduce-scatter.2.cloned.1.call-update
  24.9 0.1 reshape.103
  25.0 0.0 copy-done.6
  25.0 0.6 dynamic-slice
  26.3 79.0 %all-reduce.2 = f32[256,32]{1,0:T(8,128)S(1)} all-reduce(f32[256,32]{1,0:T(8,128)S(1)} %reshape.103), channel_id=3, replica_groups=mesh['dp'=16,'node'=4,'pipe'=4] {'dp','node','pipe'}, use_global_device_ids=true, to_apply=%region_5.6.clone | all-reduce | flops 8192 | bytes 65536
  105.3 0.0 copy-done.3
  105.3 0.0 copy-done.4
  105.3 1.2 subtract_convert_fusion.1
  106.5 0.2 dynamic-update-slice
  106.7 11.5 all-reduce.1
  118.3 1176.1 %reduce-scatter.2.cloned.1.call-done = f32[1,32,128]{2,1,0:T(8,128)} async-done(((f32[256,32,128]{2,1,0:T(8,128)}), f32[1,32,128]{2,1,0:T(8,128)}) %reduce-scatter.2.cloned.1.call-update) | async-done | bytes 16400 | tf_op jit(solution)/shard_map/reduce_scatter | solution.py:119
  1294.4 0.0 copy-done.1
  1294.4 0.0 copy-done.2
  1294.4 1.4 subtract_convert_fusion
  1295.8 11.9 all_gather.6
  1307.7 0.6 copy.20
  (7 shorter events, 0.1 us)
Async XLA Ops:
  7.2 10.6 copy-start
  7.2 1287.3 %reduce-scatter.2.cloned.1.call-start = ((), (), s32[]{:S(2)}) async-start(), calls=%async_computation.1 | async-start | bytes 4210688 | tf_op jit(solution)/shard_map/reduce_scatter | solution.py:119
  12.6 5.2 copy-start.5
  22.3 2.7 copy-start.6
  22.3 83.0 %copy-start.3 = (f32[32]{0:T(128)S(1)}, f32[32]{0:T(128)}, u32[]{:S(2)}) copy-start(f32[32]{0:T(128)} %param.22) | copy-start | bytes 388
  22.3 83.0 %copy-start.4 = (f32[32]{0:T(128)S(1)}, f32[32]{0:T(128)}, u32[]{:S(2)}) copy-start(f32[32]{0:T(128)} %param.23) | copy-start | bytes 388
  22.3 1272.1 %copy-start.1 = (f32[32,128]{1,0:T(8,128)S(1)}, f32[32,128]{1,0:T(8,128)}, u32[]{:S(2)}) copy-start(f32[32,128]{1,0:T(8,128)} %param.20) | copy-start | bytes 49156
  22.4 1272.1 %copy-start.2 = (f32[32,128]{1,0:T(8,128)S(1)}, f32[32,128]{1,0:T(8,128)}, u32[]{:S(2)}) copy-start(f32[32,128]{1,0:T(8,128)} %param.21) | copy-start | bytes 49156
Sparse Core Ops, SparseCore 0:
  25.0 1269.3 reduce-scatter.1
where the time goes:
time: 1320 us
  waiting for transfers between devices  1180 us (89%)
  blocking collectives  102 us (8%)
  between operations  14.9 us (1%)
    reduce_scatter x1, waiting for transfers between devices, shards(): lax.psum_scatter(summed[0], ('dp', 'node', 'pipe'), scatter_dimension=0,...  1180 us
    unnamed x2, blocking collectives  90.6 us
  transfers between devices with their start and end apart: 1, of which 1 were waited for; matrix products, arithmetic and copies ran while one was open for 0% of the time, Pallas kernels for 0%

commit v1 on v0

--- a/solution.py
+++ b/solution.py
@@ -50,17 +50,22 @@
     return (traced + value_rows).reshape(-1)
 
 
-def local_terms(hidden, gain, head, targets, mask, row_scale_exp, block_scale_exp):
+def forward(hidden, gain, head, targets, mask):
     hidden_f = hidden.astype(jnp.float32)
     inv_rms = lax.rsqrt(jnp.mean(hidden_f * hidden_f, axis=1, keepdims=True) + NORM_EPSILON)
-    normed = hidden_f * inv_rms
-    scaled = (normed * gain.astype(jnp.float32)).astype(jnp.bfloat16)
+    scaled = (hidden_f * inv_rms * gain.astype(jnp.float32)).astype(jnp.bfloat16)
     logits = LOGIT_SCALE * jnp.dot(scaled, head, preferred_element_type=jnp.float32)
     shifted = jnp.exp(logits - jnp.max(logits, axis=1, keepdims=True))
     probs_out = shifted / jnp.sum(shifted, axis=1, keepdims=True)
     errors = (LOGIT_SCALE * mask.astype(jnp.float32)[:, None] * (probs_out - targets)).astype(
         jnp.bfloat16
     )
+    return errors, inv_rms
+
+
+def group_grads(hidden, inv_rms, errors, gain, head, row_scale_exp, block_scale_exp):
+    normed = hidden.astype(jnp.float32) * inv_rms
+    scaled = (normed * gain.astype(jnp.float32)).astype(jnp.bfloat16)
     weight_part = lax.dot_general(
         scaled, errors, (((0,), (0,)), ((), ())), preferred_element_type=jnp.float32
     )
@@ -72,8 +77,7 @@
     block_limit = SAT_LIMIT * jnp.repeat(jnp.exp2(block_scale_exp.astype(jnp.float32)), GBLK)
     weight_q = jnp.clip(weight_part, -row_limit[:, None], row_limit[:, None]).astype(jnp.bfloat16)
     gain_q = jnp.clip(gain_part, -block_limit, block_limit).astype(jnp.bfloat16)
-    weight_q, gain_q = lax.optimization_barrier((weight_q, gain_q))
-    return (weight_q.astype(jnp.float32), gain_q.astype(jnp.float32))
+    return weight_q.astype(jnp.float32), gain_q.astype(jnp.float32)
 
 
 def adam_update(param, grad, first, second):
@@ -101,37 +105,79 @@
     first_g,
     second_g,
 ):
-    targets = gauss_targets(gae_returns(rewards, old_values))
-    weight_q, gain_q = local_terms(
-        final_hidden, norm_gain, value_head, targets, loss_mask, row_exp[0], gain_exp[0]
-    )
     size_dp = lax.axis_size("dp")
     size_node = lax.axis_size("node")
     size_pipe = lax.axis_size("pipe")
-    row_count = first_g.shape[0]
-    bin_count = value_head.shape[1]
-    total_groups = size_dp * size_node * size_pipe
-    summed = (
-        weight_q.reshape(total_groups, row_count, bin_count),
-        gain_q.reshape(total_groups, row_count),
-    )
-    summed = (
-        lax.psum_scatter(summed[0], ("dp", "node", "pipe"), scatter_dimension=0, tiled=True),
-        lax.psum_scatter(summed[1], ("dp", "node", "pipe"), scatter_dimension=0, tiled=True),
-    )
-    grad_w = summed[0].reshape(row_count, bin_count)
-    grad_g = summed[1].reshape(row_count)
+    size_z = size_dp // 2
+    size_xy = size_node * size_pipe
+    rows = first_g.shape[0]
+    bins = value_head.shape[1]
+    tokens = final_hidden.shape[0]
+    core = lax.rem(lax.axis_index("dp"), 2)
+    swap = [(i, i ^ 1) for i in range(size_dp)]
+    same_core = [[c + 2 * i for i in range(size_z)] for c in range(2)]
+    span = size_xy * rows
+
+    def half(values, side):
+        lead = values.shape[:-1]
+        parts = values.reshape(*lead, size_z, 2, values.shape[-1] // (2 * size_z))
+        return lax.dynamic_index_in_dim(parts, side, len(lead) + 1, keepdims=False).reshape(
+            *lead, values.shape[-1] // 2
+        )
+
+    other_hidden = lax.ppermute(half(final_hidden, 1 - core), "dp", swap)
+    other_row_exp = lax.ppermute(half(row_exp[0], 1 - core), "dp", swap)
+    other_gain_exp = lax.ppermute(half(gain_exp[0], 1 - core), "dp", swap)
+
+    targets = gauss_targets(gae_returns(rewards, old_values))
+    errors, inv_rms = forward(final_hidden, norm_gain, value_head, targets, loss_mask)
+    other_errors = lax.ppermute(errors, "dp", swap)
+    other_rms = lax.ppermute(inv_rms, "dp", swap)
+
+    own_gain = half(norm_gain, core)
+    own_head = half(value_head.T, core).T
+    mine = group_grads(
+        half(final_hidden, core), inv_rms, errors, own_gain, own_head,
+        half(row_exp[0], core), half(gain_exp[0], core),
+    )
+    theirs = group_grads(
+        other_hidden, other_rms, other_errors, own_gain, own_head, other_row_exp, other_gain_exp
+    )
+    weight_pair = (mine[0] + theirs[0]).astype(jnp.bfloat16)
+    weight_pair = weight_pair.reshape(size_z, size_xy, rows, bins).transpose(1, 0, 2, 3)
+    weight_pair = weight_pair.reshape(size_xy, size_z * rows, bins)
+    gain_pair = (mine[1] + theirs[1]).reshape(size_z, size_xy, rows).transpose(1, 0, 2)
+    gain_pair = gain_pair.reshape(size_xy, size_z * rows // bins, bins)
+    gain_high = gain_pair.astype(jnp.bfloat16)
+    gain_low = (gain_pair - gain_high.astype(jnp.float32)).astype(jnp.bfloat16)
+    filler = jnp.zeros((size_xy, 12, bins), jnp.bfloat16)
+    packed = jnp.concatenate([weight_pair, gain_high, gain_low, filler], axis=1)
+    packed = lax.all_to_all(packed, ("node", "pipe"), 0, 0, tiled=True)
+    plane = jnp.sum(packed.astype(jnp.float32), axis=0)
+    plane_w = plane[: size_z * rows].reshape(size_z, rows, bins)
+    plane_g = plane[size_z * rows :][:2] + plane[size_z * rows :][2:4]
+    plane_g = jnp.pad(plane_g.reshape(size_z, 1, rows), ((0, 0), (0, 7), (0, bins - rows)))
+    packed = jnp.concatenate([plane_w, plane_g], axis=1)
+    packed = lax.all_to_all(packed, "dp", 0, 0, tiled=True, axis_index_groups=same_core)
+    total = jnp.sum(packed, axis=0)
+    grad_w = total[:rows]
+    grad_g = total[rows, :rows]
+
     position = (
         lax.axis_index("dp") * size_node + lax.axis_index("node")
     ) * size_pipe + lax.axis_index("pipe")
-    own_weight = lax.dynamic_slice_in_dim(value_head, position * row_count, row_count, 0)
-    own_gain = lax.dynamic_slice_in_dim(norm_gain, position * row_count, row_count, 0)
+    own_weight = lax.dynamic_slice_in_dim(value_head, position * rows, rows, 0)
+    own_gain = lax.dynamic_slice_in_dim(norm_gain, position * rows, rows, 0)
     shard_weight, first_w_new, second_w_new = adam_update(own_weight, grad_w, first_w, second_w)
     shard_gain, first_g_new, second_g_new = adam_update(own_gain, grad_g, first_g, second_g)
-    new_weight, new_gain = (
-        lax.all_gather(shard_weight, "pipe", axis=0, tiled=True),
-        lax.all_gather(shard_gain, "pipe", axis=0, tiled=True),
-    )
+    packed = jnp.concatenate(
+        [shard_weight, jnp.pad(shard_gain[None], ((0, 7), (0, bins - rows)))], axis=0
+    )
+    packed = lax.all_to_all(
+        jnp.broadcast_to(packed, (size_pipe, *packed.shape)), "pipe", 0, 0, tiled=True
+    )
+    new_weight = packed[:, :rows].reshape(size_pipe * rows, bins)
+    new_gain = packed[:, rows, :rows].reshape(size_pipe * rows)
     return (new_weight, new_gain, first_w_new, second_w_new, first_g_new, second_g_new)
 
 

time: 1320 us -> 89.4 us (0.07)
  waiting for transfers between devices: 1180 us -> 9.44 us
  blocking collectives: 102 us -> 32.1 us
  local copies, waits for them, and re-layouts: 3.15 us -> 18.8 us
  between operations: 14.9 us -> 1.1 us
    reduce_scatter x1 -> x0, waiting for transfers between devices: 1180 us -> none  [shards(): lax.psum_scatter(summed[0], ('dp', 'node', 'pipe'), scatter_dimension=0,...]
    unnamed x2 -> x0, blocking collectives: 90.6 us -> none
    all_to_all x0 -> x2, blocking collectives: none -> 32.1 us  [the longest x1 24.1 us: shards(): packed = lax.all_to_all(packed, ('node', 'pipe'), 0, 0, tiled=True)]
  transfers between devices with their start and end apart: 1 -> 6, of which waited for: 1 -> 1; matrix products, arithmetic and copies ran while one was open for 0% -> 15% of each run, Pallas kernels for 0% -> 0%
where the time goes in v1:
time: 89.4 us; the launch traced here: 88.9 us
  blocking collectives  32.1 us (36%)
  local copies, waits for them, and re-layouts  18.8 us (21%)
  matrix products  10.7 us (12%)
  starting transfers between devices  9.67 us (11%)
  waiting for transfers between devices  9.44 us (11%)
  other arithmetic  7.12 us (8%)
  between operations  1.1 us (1%)
    all_to_all x1, blocking collectives, shards(): packed = lax.all_to_all(packed, ('node', 'pipe'), 0, 0, tiled=True)  24.1 us
    all_to_all x1, waiting for transfers between devices, shards(): lax.all_to_all(packed, 'dp', 0, 0, tiled=True, axis_index_groups=same_core)  9.43 us
    dynamic_slice x4, local copies, waits for them, and re-layouts, half(): lax.dynamic_index_in_dim(parts, side, len(lead) + 1, keepdims=False)  8.47 us
    all_to_all x1, starting transfers between devices, shards(): lax.all_to_all(packed, 'dp', 0, 0, tiled=True, axis_index_groups=same_core)  8.46 us
    all_to_all x1, blocking collectives, shards(): lax.all_to_all(jnp.broadcast_to(packed, (size_pipe, *packed.shape)), 'pip...  7.95 us
    dot_general x2, matrix products, group_grads(): lax.dot_general(scaled, errors, (((0,), (0,)), ((), ())), preferred_eleme...  5.45 us
    unnamed x31, local copies, waits for them, and re-layouts  4.23 us
    reshape x2, local copies, waits for them, and re-layouts, half(): parts = values.reshape(*lead, size_z, 2, values.shape[-1] // (2 * size_z))  3.31 us
  transfers between devices with their start and end apart: 6, of which 1 were waited for; matrix products, arithmetic and copies ran while one was open for 15% of the time, Pallas kernels for 0%

profile of v1, /device:TPU:2, one launch (start us, length us, event | category | flops | bytes accessed | tf_op | source)
XLA Modules:
  0.0 88.9 jit_solution(10411939803398011292)
XLA Ops:
  0.6 3.3 %reshape.166 = bf16[128,8,2,512]{3,2,1,0:T(2,128)(2,1)S(1)} reshape(bf16[128,8192]{1,0:T(8,128)(2,1)} %param.12) | data formatting | bytes 4194304 | tf_op jit(solution)/shard_map/reshape | solution.py:123
  4.0 8.3 %dynamic-slice_reduce_fusion = (bf16[128,8,512]{2,1,0:T(8,128)(2,1)S(1)}, bf16[128,8,1,512]{3,2,1,0:T(2,128)(2,1)}) fusion(bf16[128,8,2,512]{3,2,1,0:T(2,128)(2,1)S(1)} %reshape.166, s32[]{:T(128)S(6)} %select_n.27, s32[]{:T(128)S(6)} %select_n.25), kind=kLoop, calls=%fused_computation.18 | loop fusion | bytes 4194312 | tf_op jit(solution)/shard_map/jit(dynamic_index_in_dim)/dynamic_slice | solution.py:124
  12.4 1.4 %copy.95 = bf16[16,8,8,512]{3,1,2,0:T(8,128)(2,1)} copy(bf16[16,8,8,512]{3,2,1,0:T(8,128)(2,1)S(1)} %bitcast.57) | data formatting | bytes 2097152
  13.7 0.5 copy-done
  14.3 0.5 fusion.3
  14.8 0.1 reshape.169
  14.9 0.1 reshape.168
  15.0 0.1 fusion.15
  15.2 0.1 min.42
  15.3 0.1 add_multiply_fusion
  15.4 2.7 %fusion.52 = (f32[128]{0:T(128)S(1)}, f32[128,128]{0,1:T(8,128)S(1)}) fusion(bf16[8192,128]{1,0:T(8,128)(2,1)} %param.13, bf16[128,8192]{1,0:T(8,128)(2,1)S(1)} %copy-done, f32[8192]{0:T(1024)S(1)} %convert_element_type.141, f32[128]{0:T(128)S(1)} %get-tuple-element.23), kind=kOutput, calls=%fused_computation.99 | convolution fusion | flops 272662400 | bytes 4293632 | tf_op jit(solution)/shard_map/dot_general | solution.py:57
  18.2 0.1 collective-permute-start.3
  18.3 0.5 collective-permute-start.2
  18.8 0.5 broadcast.167
  19.3 0.7 reduce.14
  20.0 0.1 reshape_squeeze.12
  20.2 0.1 collective-permute-start.4
  20.3 0.7 reduce.15
  21.1 0.5 collective-permute-start
  21.6 0.1 copy.92
  21.8 1.8 %copy_convert_fusion = f32[128,8,1,512]{3,1,0,2:T(8,128)S(1)} fusion(bf16[128,8,1,512]{3,2,1,0:T(2,128)(2,1)} %get-tuple-element.15), kind=kLoop, calls=%fused_computation.28 | loop fusion | flops 524288 | bytes 3145728 | tf_op jit(solution)/shard_map/convert_element_type | solution.py:67
  23.7 1.7 %copy.94 = f32[16,8,8,512]{3,1,2,0:T(8,128)S(1)} copy(f32[16,8,8,512]{3,2,1,0:T(8,128)S(1)} %bitcast.52) | data formatting | bytes 4194304
  25.3 0.1 constant_dynamic-slice_fusion
  25.4 0.5 fusion.10
  25.9 0.1 reduce_sum.61
  26.0 0.1 copy.84
  26.1 2.7 %fusion.2 = f32[4096,128]{1,0:T(8,128)} fusion(bf16[128,128]{0,1:T(8,128)(2,1)S(1)} %fusion.23, f32[128,4096]{1,0:T(8,128)S(1)} %bitcast.51, f32[4096]{0:T(1024)S(1)} %bitcast.60, f32[128]{0:T(128)S(1)} %get-tuple-element.23, bf16[4096]{0:T(1024)(128)(2,1)S(1)} %neg.22, f32[4096]{0:T(1024)S(1)} %bitcast.63), kind=kOutput, calls=%fused_computation.8 | convolution fusion | flops 138412032 | bytes 4268544 | tf_op jit(solution)/shard_map/dot_general | solution.py:69
  29.0 0.1 mul.246
  29.0 0.1 copy.85
  29.2 0.1 copy.87
  29.4 1.9 %fusion.11 = bf16[4096]{0:T(1024)(128)(2,1)S(1)} fusion(bf16[128,4096]{1,0:T(8,128)(2,1)} %collective-permute-done.1, bf16[128,128]{0,1:T(8,128)(2,1)S(1)} %collective-permute-done.3, bf16[128,4096]{0,1:T(8,128)(2,1)S(1)} %bitcast.55, f32[128]{0:T(128)S(1)} %bitcast.70), kind=kOutput, calls=%fused_computation.23 | convolution fusion | flops 136310784 | bytes 2138624 | tf_op jit(solution)/shard_map/dot_general | solution.py:72
  31.3 0.1 reduce_sum.63
  31.4 0.1 add_bitcast_fusion
  31.5 0.1 reshape.177
  31.7 2.7 %add_convert_fusion = bf16[4096,128]{1,0:T(8,128)(2,1)S(1)} fusion(f32[4096,128]{1,0:T(8,128)S(1)} %copy-done.1, bf16[4096]{0:T(1024)(128)(2,1)S(1)} %get-tuple-element.19, bf16[128,128]{0,1:T(8,128)(2,1)S(1)} %collective-permute-done.3, bf16[128,4096]{1,0:T(8,128)(2,1)} %collective-permute-done.1, f32[128]{0:T(128)S(1)} %bitcast.71, ...), kind=kOutput, calls=%fused_computation.14 | convolution fusion | flops 139984896 | bytes 4260352 | tf_op jit(solution)/shard_map/dot_general | solution.py:69
  34.4 0.1 copy.81
  34.5 0.3 maximum_maximum_fusion
  34.9 24.1 %all_to_all.15 = bf16[16,272,128]{2,1,0:T(8,128)(2,1)S(1)} all-to-all(bf16[16,272,128]{2,1,0:T(8,128)(2,1)S(1)} %maximum_maximum_fusion), channel_id=1, replica_groups=mesh['dp'=16,'node'=4,'pipe'=4] {'node','pipe'}, dimensions={0} | all-to-all | bytes 2228224 | tf_op jit(solution)/shard_map/all_to_all | solution.py:155
  59.0 0.2 convert_reduce_fusion
  59.2 0.1 reshape.179
  59.2 0.7 select_maximum_fusion
  59.9 8.5 %all-to-all-start.1 = ((f32[8,40,128]{2,1,0:T(8,128)}), f32[8,40,128]{2,1,0:T(8,128)S(1)}, u32[]{:S(2)}, u32[]{:S(2)}) async-start(f32[8,40,128]{2,1,0:T(8,128)} %select_maximum_fusion), calls=%async_computation.1 | async-start | bytes 327680 | tf_op jit(solution)/shard_map/all_to_all | solution.py:161
  68.4 9.4 %all-to-all-done.1 = f32[8,40,128]{2,1,0:T(8,128)S(1)} async-done(((f32[8,40,128]{2,1,0:T(8,128)}), f32[8,40,128]{2,1,0:T(8,128)S(1)}, u32[]{:S(2)}, u32[]{:S(2)}) %all-to-all-start.1) | async-done | bytes 163872 | tf_op jit(solution)/shard_map/all_to_all | solution.py:161
  77.8 0.5 convert_bitcast_fusion
  78.4 1.3 %subtract_convert_fusion = (bf16[32,128]{1,0:T(8,128)(2,1)S(1)}, f32[32,128]{1,0:T(8,128)}, f32[32,128]{1,0:T(8,128)}) fusion(bf16[8192,128]{1,0:T(8,128)(2,1)} %param.13, s32[]{:T(128)S(6)} %select_n.24, f32[40,128]{1,0:T(8,128)S(1)} %reduce_sum.65, f32[32,128]{1,0:T(8,128)S(1)} %copy-done.5, f32[32,128]{1,0:T(8,128)S(1)} %copy-done.6), kind=kLoop, calls=%fused_computation.61 | loop fusion | flops 61440 | bytes 98308 | tf_op jit(solution)/shard_map/convert_element_type | solution.py:88
  79.7 8.0 %all_to_all.16 = bf16[4,40,128]{2,1,0:T(8,128)(2,1)S(1)} all-to-all(bf16[4,40,128]{2,1,0:T(8,128)(2,1)S(1)} %broadcast_in_dim.49), channel_id=1, replica_groups=mesh['dp'=16,'node'=4,'pipe'=4] {'pipe'}, dimensions={0} | all-to-all | bytes 81920 | tf_op jit(solution)/shard_map/all_to_all | solution.py:176
  87.7 0.6 reshape_squeeze.13
  88.3 0.6 slice.61
  (67 shorter events, 0.9 us)
Async XLA Ops:
  12.3 2.0 %copy-start = (bf16[128,8192]{1,0:T(8,128)(2,1)S(1)}, bf16[128,8192]{1,0:T(8,128)(2,1)}, u32[]{:S(2)}) copy-start(bf16[128,8192]{1,0:T(8,128)(2,1)} %param.12) | copy-start | bytes 6291460
  12.3 2.5 %copy-start.7 = (f32[128]{0:T(128)S(1)}, f32[128]{0:T(128)}, u32[]{:S(2)}) copy-start(f32[128]{0:T(128)} %param.16) | copy-start | bytes 1540
  12.3 2.5 %copy-start.8 = (f32[128]{0:T(128)S(1)}, f32[128]{0:T(128)}, u32[]{:S(2)}) copy-start(f32[128]{0:T(128)} %param.15) | copy-start | bytes 1540
  12.3 2.9 %copy-start.3 = (bf16[8192]{0:T(1024)(128)(2,1)S(1)}, bf16[8192]{0:T(1024)(128)(2,1)}, u32[]{:S(2)}) copy-start(bf16[8192]{0:T(1024)(128)(2,1)} %param.14) | copy-start | bytes 49156
  12.3 3.0 %copy-start.11 = (s32[128]{0:T(128)S(1)}, s32[128]{0:T(128)}, u32[]{:S(2)}) copy-start(s32[128]{0:T(128)} %param.17) | copy-start | bytes 1540
  13.7 15.6 %collective-permute-start.1 = (bf16[128,4096]{1,0:T(8,128)(2,1)}, bf16[128,4096]{1,0:T(8,128)(2,1)}, u32[]{:S(2)}, u32[]{:S(2)}) collective-permute-start(bf16[128,4096]{1,0:T(8,128)(2,1)} %bitcast.29), channel_id=1, source_target_pairs={{0,16},{16,0},{32,48},{48,32},{64,80},{80,64},{96,112},{112,96},{1... | collective-permute-start | bytes 3145736 | tf_op jit(solution)/shard_map/ppermute | solution.py:128
  15.4 3.9 %copy-start.12 = (s32[1,64]{1,0:T(1,128)S(1)}, s32[1,64]{1,0:T(1,128)}, u32[]{:S(2)}) copy-start(s32[1,64]{1,0:T(1,128)} %param.19) | copy-start | bytes 772
  15.4 4.9 %copy-start.4 = (s32[1,8192]{1,0:T(1,128)S(1)}, s32[1,8192]{1,0:T(1,128)}, u32[]{:S(2)}) copy-start(s32[1,8192]{1,0:T(1,128)} %param.18) | copy-start | bytes 98308
  18.2 11.1 %collective-permute-start.3 = (bf16[128,128]{0,1:T(8,128)(2,1)S(1)}, bf16[128,128]{0,1:T(8,128)(2,1)S(1)}, u32[]{:S(2)}, u32[]{:S(2)}) collective-permute-start(bf16[128,128]{0,1:T(8,128)(2,1)S(1)} %fusion.23), channel_id=1, source_target_pairs={{0,16},{16,0},{32,48},{48,32},{64,80},{80,64},{96,112},{112,96},{1... | collective-permute-start | bytes 98312 | tf_op jit(solution)/shard_map/ppermute | solution.py:134
  18.3 11.0 %collective-permute-start.2 = (f32[128,1]{0,1:T(1,128)S(1)}, f32[128,1]{0,1:T(1,128)S(1)}, u32[]{:S(2)}, u32[]{:S(2)}) collective-permute-start(f32[128,1]{0,1:T(1,128)S(1)} %get-tuple-element.22), channel_id=1, source_target_pairs={{0,16},{16,0},{32,48},{48,32},{64,80},{80,64},{96,112},{112,96},{1... | collective-permute-start | bytes 1544 | tf_op jit(solution)/shard_map/ppermute | solution.py:135
  20.2 8.8 %collective-permute-start.4 = (s32[32]{0:T(128)S(1)}, s32[32]{0:T(128)S(1)}, u32[]{:S(2)}, u32[]{:S(2)}) collective-permute-start(s32[32]{0:T(128)S(1)} %reshape.176), channel_id=1, source_target_pairs={{0,16},{16,0},{32,48},{48,32},{64,80},{80,64},{96,112},{112,96},{1... | collective-permute-start | bytes 392 | tf_op jit(solution)/shard_map/ppermute | solution.py:130
  21.1 8.2 %collective-permute-start = (s32[4096]{0:T(1024)S(1)}, s32[4096]{0:T(1024)S(1)}, u32[]{:S(2)}, u32[]{:S(2)}) collective-permute-start(s32[4096]{0:T(1024)S(1)} %bitcast.69), channel_id=1, source_target_pairs={{0,16},{16,0},{32,48},{48,32},{64,80},{80,64},{96,112},{112,96},{1... | collective-permute-start | bytes 49160 | tf_op jit(solution)/shard_map/ppermute | solution.py:129
  23.6 1.7 %copy-start.2 = (bf16[8192,128]{1,0:T(8,128)(2,1)S(1)}, bf16[8192,128]{1,0:T(8,128)(2,1)}, u32[]{:S(2)}) copy-start(bf16[8192,128]{1,0:T(8,128)(2,1)} %param.13) | copy-start | bytes 6291460
  28.9 2.8 %copy-start.1 = (f32[4096,128]{1,0:T(8,128)S(1)}, f32[4096,128]{1,0:T(8,128)}, u32[]{:S(2)}) copy-start(f32[4096,128]{1,0:T(8,128)} %fusion.2) | copy-start | bytes 6291460
  34.8 43.0 %copy-start.9 = (f32[32]{0:T(128)S(1)}, f32[32]{0:T(128)}, u32[]{:S(2)}) copy-start(f32[32]{0:T(128)} %param.22) | copy-start | bytes 388
  34.8 43.0 %copy-start.10 = (f32[32]{0:T(128)S(1)}, f32[32]{0:T(128)}, u32[]{:S(2)}) copy-start(f32[32]{0:T(128)} %param.23) | copy-start | bytes 388
  34.8 43.5 %copy-start.5 = (f32[32,128]{1,0:T(8,128)S(1)}, f32[32,128]{1,0:T(8,128)}, u32[]{:S(2)}) copy-start(f32[32,128]{1,0:T(8,128)} %param.20) | copy-start | bytes 49156
  34.9 43.5 %copy-start.6 = (f32[32,128]{1,0:T(8,128)S(1)}, f32[32,128]{1,0:T(8,128)}, u32[]{:S(2)}) copy-start(f32[32,128]{1,0:T(8,128)} %param.21) | copy-start | bytes 49156
  59.9 17.9 %all-to-all-start.1 = ((f32[8,40,128]{2,1,0:T(8,128)}), f32[8,40,128]{2,1,0:T(8,128)S(1)}, u32[]{:S(2)}, u32[]{:S(2)}) async-start(f32[8,40,128]{2,1,0:T(8,128)} %select_maximum_fusion), calls=%async_computation.1 | async-start | bytes 327680 | tf_op jit(solution)/shard_map/all_to_all | solution.py:161

commit v2 on v0

v2 whole, which is shorter than its diff:
```python
import math

import jax
import jax.numpy as jnp
from jax import lax
from jax.experimental import pallas as pl
from jax.experimental.pallas import tpu as pltpu
from jax.sharding import PartitionSpec as P

BINS = 128
GBLK = 128
SEQ = 32


LOGIT_SCALE = 0.0625
RETURN_LOW = -4.0
RETURN_HIGH = 4.0
TRACE_DECAY = 0.95
SAT_LIMIT = 448.0
LEARN_RATE = 0.02
FIRST_CORR = 0.19
SECOND_CORR = 0.0975
EPSILON = 1e-08
NORM_EPSILON = 1e-06


LANES = 128
CHUNKS = 8
LIMIT_BASE = 16


def limit_of(exponent):
    power = jnp.left_shift(jnp.ones_like(exponent), exponent + LIMIT_BASE)
    return power.astype(jnp.float32) * (SAT_LIMIT * 2.0**-LIMIT_BASE)


def target_mass(rewards, old_values, tokens):
    width = (RETURN_HIGH - RETURN_LOW) / BINS
    scale = 0.75 * width * math.sqrt(2.0)
    token = lax.broadcasted_iota(jnp.int32, (tokens, tokens), 0)
    later = lax.broadcasted_iota(jnp.int32, (tokens, tokens), 1)
    values = jnp.broadcast_to(old_values, (tokens, tokens))
    following = jnp.where(lax.rem(later, SEQ) == SEQ - 1, 0.0, pltpu.roll(values, tokens - 1, 1))
    td_error = rewards + following - values
    behind = (later - token).astype(jnp.float32)
    inside = jnp.logical_and(later >= token, lax.div(later, SEQ) == lax.div(token, SEQ))
    decay = jnp.where(inside, jnp.exp(jnp.maximum(behind, 0.0) * math.log(TRACE_DECAY)), 0.0)
    own = jnp.where(later == token, values, 0.0)
    returns = jnp.sum(decay * td_error + own, axis=1, keepdims=True)
    returns = jnp.clip(returns, RETURN_LOW, RETURN_HIGH)
    edge = lax.broadcasted_iota(jnp.int32, (tokens, BINS), 1).astype(jnp.float32) * width
    edge = edge + RETURN_LOW
    below = 0.5 * (1.0 + lax.erf((edge - returns) / scale))
    above = 0.5 * (1.0 + lax.erf((edge + width - returns) / scale))
    return (above - below) / (above[:, BINS - 1 :] - below[:, :1])


def forward_kernel(
    gain_exp, hidden, head, gain, rewards, old_values, mask, row_exp, pack, hidden_v, head_v, sems
):
    tokens, width = hidden.shape
    span = width // CHUNKS
    copies = []
    for n in range(CHUNKS):
        copies.append(
            pltpu.make_async_copy(
                hidden.at[:, n * span : (n + 1) * span], hidden_v.at[n], sems.at[n]
            )
        )
    for n in range(CHUNKS):
        copies.append(
            pltpu.make_async_copy(
                head.at[n * span : (n + 1) * span, :], head_v.at[n], sems.at[CHUNKS + n]
            )
        )
    for copy in copies:
        copy.start()
    blocks = width // LANES
    for n in range(blocks):
        pack[2 * tokens + n : 2 * tokens + n + 1, :] = limit_of(
            row_exp[:, n * LANES : (n + 1) * LANES]
        )
        pack[2 * tokens + blocks + n : 2 * tokens + blocks + n + 1, :] = limit_of(
            jnp.full((1, LANES), gain_exp[0, n], jnp.int32)
        )
    targets = target_mass(rewards[...], old_values[...], tokens)
    row = lax.broadcasted_iota(jnp.int32, (tokens, tokens), 0)
    column = lax.broadcasted_iota(jnp.int32, (tokens, tokens), 1)
    counted = jnp.where(row == column, mask[...].astype(jnp.float32), 0.0)
    counted = jnp.sum(counted, axis=1, keepdims=True)
    square = jnp.zeros((tokens, LANES), jnp.float32)
    for n in range(CHUNKS):
        copies[n].wait()
        part = hidden_v[n].astype(jnp.float32)
        part = part * part
        for m in range(span // LANES):
            square = square + part[:, m * LANES : (m + 1) * LANES]
    inv_rms = lax.rsqrt(jnp.sum(square, axis=1, keepdims=True) / width + NORM_EPSILON)
    gains = gain[...].astype(jnp.float32)
    logits = jnp.zeros((tokens, BINS), jnp.float32)
    for n in range(CHUNKS):
        copies[CHUNKS + n].wait()
        first = n * span // LANES
        gain_row = jnp.concatenate(
            [gains[first + m : first + m + 1, :] for m in range(span // LANES)], axis=1
        )
        normed = hidden_v[n].astype(jnp.float32) * inv_rms
        scaled = (normed * gain_row).astype(jnp.bfloat16)
        logits = logits + jnp.dot(scaled, head_v[n], preferred_element_type=jnp.float32)
    logits = LOGIT_SCALE * logits
    shifted = jnp.exp(logits - jnp.max(logits, axis=1, keepdims=True))
    probs = shifted / jnp.sum(shifted, axis=1, keepdims=True)
    errors = (LOGIT_SCALE * counted * (probs - targets)).astype(jnp.bfloat16)
    pack[:tokens, :] = errors.astype(jnp.float32)
    pack[tokens : 2 * tokens, :] = jnp.broadcast_to(inv_rms, (tokens, LANES))


def run_forward(hidden, head, gain, rewards, old_values, mask, row_exp, gain_exp):
    tokens, width = hidden.shape
    span = width // CHUNKS
    rows = 2 * tokens + 2 * (width // LANES)
    anywhere = pl.BlockSpec(memory_space=pl.ANY)
    vmem = pl.BlockSpec(memory_space=pltpu.VMEM)
    return pl.pallas_call(
        forward_kernel,
        out_shape=jax.ShapeDtypeStruct((rows, LANES), jnp.float32),
        in_specs=[pl.BlockSpec(memory_space=pltpu.SMEM), anywhere, anywhere] + [vmem] * 5,
        out_specs=vmem,
        scratch_shapes=[
            pltpu.VMEM((CHUNKS, tokens, span), jnp.bfloat16),
            pltpu.VMEM((CHUNKS, span, BINS), jnp.bfloat16),
            pltpu.SemaphoreType.DMA((2 * CHUNKS,)),
        ],
        cost_estimate=pl.CostEstimate(
            flops=2 * tokens * width * BINS, bytes_accessed=8 * width * tokens, transcendentals=0
        ),
        compiler_params=pltpu.CompilerParams(vmem_limit_bytes=63 * 2**20),
        name="forward",
    )(
        gain_exp,
        hidden,
        head,
        gain,
        rewards,
        old_values,
        mask,
        row_exp,
    )


def grads_kernel(
    place, hidden, other, head, gain, pack, other_pack, first_w, second_w, first_g, second_g,
    out, moments, hidden_v, head_v, gain_f, gain_sum, sems,
):
    tokens, width = hidden.shape
    size_z, span = head_v.shape[0], head_v.shape[1]
    tiles = span // LANES
    rows = span // out.shape[0]
    side = place[0]
    copies = []
    for z in range(size_z):
        start = pl.multiple_of((2 * z + side) * span, span)
        copies.append(
            (
                pltpu.make_async_copy(
                    hidden.at[:, pl.ds(start, span)], hidden_v.at[0, z], sems.at[0, z]
                ),
                pltpu.make_async_copy(
                    other.at[:, pl.ds(start, span)], hidden_v.at[1, z], sems.at[1, z]
                ),
                pltpu.make_async_copy(head.at[pl.ds(start, span), :], head_v.at[z], sems.at[2, z]),
            )
        )
        for copy in copies[-1]:
            copy.start()
    gain_f[...] = gain[...].astype(jnp.float32)
    owner = lax.broadcasted_iota(jnp.int32, (1, LANES), 1) // rows == place[1]
    moments[:rows, :] = first_w[...]
    moments[rows : 2 * rows, :] = second_w[...]
    for n, values in enumerate((first_g, second_g)):
        repeated = jnp.concatenate([values[...]] * (LANES // rows), axis=1)
        moments[2 * rows + n : 2 * rows + n + 1, :] = jnp.where(owner, repeated, 0.0)
    moments[2 * rows + 2 :, :] = jnp.zeros((6, LANES), jnp.float32)
    packs = (pack, other_pack)
    errors = [p[:tokens, :] for p in packs]
    flipped = [e.T.astype(jnp.bfloat16) for e in errors]
    errors = [e.astype(jnp.bfloat16) for e in errors]
    inv_rms = [jnp.concatenate([p[tokens : 2 * tokens, :]] * tiles, axis=1) for p in packs]
    blocks = width // LANES

    def spread(ref, first):
        return jnp.concatenate([ref[pl.ds(first + m, 1), :] for m in range(tiles)], axis=1)

    for z in range(size_z):
        for copy in copies[z]:
            copy.wait()
        first = (2 * z + side) * tiles
        gain_row = spread(gain_f, first)
        weight = jnp.zeros((BINS, span), jnp.float32)
        total = jnp.zeros((1, span), jnp.float32)
        for g in range(2):
            normed = hidden_v[g, z].astype(jnp.float32) * inv_rms[g]
            scaled = (normed * gain_row).astype(jnp.bfloat16)
            back = lax.dot_general(
                errors[g], head_v[z], (((1,), (1,)), ((), ())), preferred_element_type=jnp.float32
            )
            gain_part = jnp.sum(back * normed, axis=0, keepdims=True)
            limit = spread(packs[g], 2 * tokens + blocks + first)
            gain_q = jnp.clip(gain_part, -limit, limit).astype(jnp.bfloat16)
            total = total + gain_q.astype(jnp.float32)
            part = jnp.dot(flipped[g], scaled, preferred_element_type=jnp.float32)
            limit = spread(packs[g], 2 * tokens + first)
            weight_q = jnp.clip(part, -limit, limit).astype(jnp.bfloat16)
            weight = weight + weight_q.astype(jnp.float32)
        weight = weight.astype(jnp.bfloat16)
        for m in range(tiles):
            lanes = slice(m * LANES, (m + 1) * LANES)
            turned = weight[:, lanes].T
            gain_sum[m, z : z + 1, :] = total[:, lanes]
            for n in range(LANES // rows):
                out[m * (LANES // rows) + n, z * rows : (z + 1) * rows, :] = turned[
                    n * rows : (n + 1) * rows, :
                ]
    for m in range(tiles):
        high = gain_sum[m].astype(jnp.bfloat16)
        low = (gain_sum[m] - high.astype(jnp.float32)).astype(jnp.bfloat16)
        both = jnp.concatenate([high.astype(jnp.float32), low.astype(jnp.float32)], axis=0)
        for n in range(LANES // rows):
            out[m * (LANES // rows) + n, size_z * rows :, :] = both.astype(jnp.bfloat16)


def run_grads(place, hidden, other, head, gain, packs, moments, size_z, size_xy):
    tokens, width = hidden.shape
    span = width // (2 * size_z)
    rows = span // size_xy
    anywhere = pl.BlockSpec(memory_space=pl.ANY)
    vmem = pl.BlockSpec(memory_space=pltpu.VMEM)
    return pl.pallas_call(
        grads_kernel,
        out_shape=(
            jax.ShapeDtypeStruct((size_xy, size_z * rows + 2 * size_z, BINS), jnp.bfloat16),
            jax.ShapeDtypeStruct((2 * rows + 8, LANES), jnp.float32),
        ),
        in_specs=[pl.BlockSpec(memory_space=pltpu.SMEM), anywhere, anywhere, anywhere] + [vmem] * 7,
        out_specs=(vmem, vmem),
        scratch_shapes=[
            pltpu.VMEM((2, size_z, tokens, span), jnp.bfloat16),
            pltpu.VMEM((size_z, span, BINS), jnp.bfloat16),
            pltpu.VMEM((width // LANES, LANES), jnp.float32),
            pltpu.VMEM((span // LANES, size_z, LANES), jnp.float32),
            pltpu.SemaphoreType.DMA((3, size_z)),
        ],
        cost_estimate=pl.CostEstimate(
            flops=4 * tokens * width * BINS, bytes_accessed=8 * width * tokens, transcendentals=0
        ),
        compiler_params=pltpu.CompilerParams(vmem_limit_bytes=60 * 2**20),
        name="grads",
    )(place, hidden, other, head, gain, *packs, *moments)


def plane_kernel(parts, out):
    size_z = (parts.shape[1] - 2 * 8) // 32
    copies = out.shape[0] // size_z
    rows = 32
    total = parts[0].astype(jnp.float32)
    for n in range(1, parts.shape[0]):
        total = total + parts[n].astype(jnp.float32)
    for z in range(size_z):
        high_row = size_z * rows + z
        low_row = high_row + size_z
        gain = total[high_row : high_row + 1, :] + total[low_row : low_row + 1, :]
        high = gain.astype(jnp.bfloat16).astype(jnp.float32)
        block = jnp.concatenate(
            [
                total[z * rows : (z + 1) * rows, :],
                high,
                gain - high,
                jnp.zeros((6, LANES), jnp.float32),
            ],
            axis=0,
        ).astype(jnp.bfloat16)
        for n in range(copies):
            out[z * copies + n] = block


def run_plane(parts, size_z, size_pipe):
    vmem = pl.BlockSpec(memory_space=pltpu.VMEM)
    return pl.pallas_call(
        plane_kernel,
        out_shape=jax.ShapeDtypeStruct((size_z * size_pipe, 40, LANES), jnp.bfloat16),
        in_specs=[vmem],
        out_specs=vmem,
        compiler_params=pltpu.CompilerParams(vmem_limit_bytes=12 * 2**20),
        name="plane",
    )(parts)


def adam(param, grad, first, second):
    first_new = 0.9 * first + 0.1 * grad
    second_new = 0.95 * second + 0.05 * grad * grad
    update = first_new / FIRST_CORR / (jnp.sqrt(second_new / SECOND_CORR) + EPSILON)
    return param - LEARN_RATE * update, first_new, second_new


def update_kernel(
    place, parts, head, gain, own, next_1, next_2, next_3,
    new_weight, new_gain, first_w, second_w, first_g, second_g, weight_v, gain_f, sem,
):
    rows = first_w.shape[0]
    peers = LANES // rows
    size_z = parts.shape[0] // peers
    start = pl.multiple_of(place[2] * LANES, LANES)
    copy = pltpu.make_async_copy(head.at[pl.ds(start, LANES), :], weight_v, sem)
    copy.start()
    gain_f[...] = gain[...].astype(jnp.float32)
    moments = (own, next_1, next_2, next_3)
    grad = jnp.zeros((1, LANES), jnp.float32)
    for z in range(size_z):
        block = parts[z * peers].astype(jnp.float32)
        grad = grad + (block[rows : rows + 1, :] + block[rows + 1 : rows + 2, :])
    first, second = (
        sum(m[2 * rows + n : 2 * rows + n + 1, :] for m in moments[1:])
        + moments[0][2 * rows + n : 2 * rows + n + 1, :]
        for n in range(2)
    )
    updated, first, second = adam(gain_f[pl.ds(place[2], 1), :], grad, first, second)
    new_gain[...] = updated.astype(jnp.bfloat16)
    for ref, values in ((first_g, first), (second_g, second)):
        mine = jnp.zeros((1, rows), jnp.float32)
        for n in range(peers):
            mine = jnp.where(place[1] == n, values[:, n * rows : (n + 1) * rows], mine)
        ref[...] = mine
    copy.wait()
    for n in range(peers):
        peer = lax.rem(place[1] + n, peers)
        grad = jnp.zeros((rows, BINS), jnp.float32)
        for z in range(size_z):
            grad = grad + parts[z * peers + peer].astype(jnp.float32)[:rows, :]
        at = pl.multiple_of(peer * rows, rows)
        updated, first, second = adam(
            weight_v[pl.ds(at, rows), :].astype(jnp.float32),
            grad,
            moments[n][:rows, :],
            moments[n][rows : 2 * rows, :],
        )
        new_weight[pl.ds(at, rows), :] = updated.astype(jnp.bfloat16)
        if n == 0:
            first_w[...] = first
            second_w[...] = second


def run_update(place, parts, head, gain, moments):
    vmem = pl.BlockSpec(memory_space=pltpu.VMEM)
    rows = (moments[0].shape[0] - 8) // 2
    wide = jax.ShapeDtypeStruct((rows, BINS), jnp.float32)
    thin = jax.ShapeDtypeStruct((1, rows), jnp.float32)
    return pl.pallas_call(
        update_kernel,
        out_shape=(
            jax.ShapeDtypeStruct((LANES, BINS), jnp.bfloat16),
            jax.ShapeDtypeStruct((1, LANES), jnp.bfloat16),
            wide,
            wide,
            thin,
            thin,
        ),
        in_specs=[
            pl.BlockSpec(memory_space=pltpu.SMEM),
            vmem,
            pl.BlockSpec(memory_space=pl.ANY),
        ]
        + [vmem] * 5,
        out_specs=(vmem,) * 6,
        scratch_shapes=[
            pltpu.VMEM((LANES, BINS), jnp.bfloat16),
            pltpu.VMEM(gain.shape, jnp.float32),
            pltpu.SemaphoreType.DMA,
        ],
        compiler_params=pltpu.CompilerParams(vmem_limit_bytes=12 * 2**20),
        name="update",
    )(place, parts, head, gain, *moments)


def shards(
    final_hidden,
    value_head,
    norm_gain,
    rewards,
    old_values,
    loss_mask,
    row_exp,
    gain_exp,
    first_w,
    second_w,
    first_g,
    second_g,
):
    size_dp = lax.axis_size("dp")
    size_node = lax.axis_size("node")
    size_pipe = lax.axis_size("pipe")
    size_z = size_dp // 2
    size_xy = size_node * size_pipe
    rows = first_g.shape[0]
    tokens = final_hidden.shape[0]
    blocks = value_head.shape[0] // LANES
    dp, node, pipe = (lax.axis_index(name) for name in ("dp", "node", "pipe"))
    place = jnp.stack([lax.rem(dp, 2), pipe, dp * size_node + node]).astype(jnp.int32)
    swap = [(i, i ^ 1) for i in range(size_dp)]
    columns = [
        [((2 * z + c) * size_node + x) * size_pipe + y for z in range(size_z) for y in range(size_pipe)]
        for c in range(2)
        for x in range(size_node)
    ]

    other_hidden = lax.ppermute(final_hidden, "dp", swap)
    gain_blocks = norm_gain.reshape(blocks, LANES)
    pack = run_forward(
        final_hidden,
        value_head,
        gain_blocks,
        rewards.reshape(1, tokens),
        old_values.reshape(1, tokens),
        loss_mask.reshape(1, tokens),
        row_exp,
        gain_exp,
    )
    other_pack = lax.ppermute(pack, "dp", swap)
    packed, moments = run_grads(
        place,
        final_hidden,
        other_hidden,
        value_head,
        gain_blocks,
        (pack, other_pack),
        (first_w, second_w, first_g.reshape(1, rows), second_g.reshape(1, rows)),
        size_z,
        size_xy,
    )
    packed = lax.all_to_all(packed, ("node", "pipe"), 0, 0, tiled=True)
    moments = [moments] + [
        lax.ppermute(moments, "pipe", [(i, (i - k) % size_pipe) for i in range(size_pipe)])
        for k in range(1, size_pipe)
    ]
    packed = run_plane(packed, size_z, size_pipe)
    packed = lax.all_to_all(
        packed, ("dp", "node", "pipe"), 0, 0, tiled=True, axis_index_groups=columns
    )
    new_weight, new_gain, first_w, second_w, first_g, second_g = run_update(
        place, packed, value_head, gain_blocks, moments
    )
    return (
        new_weight,
        new_gain.reshape(size_pipe * rows),
        first_w,
        second_w,
        first_g.reshape(rows),
        second_g.reshape(rows),
    )


def solution(mesh):
    return jax.shard_map(
        shards,
        mesh=mesh,
        in_specs=(
            P(("dp", "node", "pipe"), None),
            P(),
            P(),
            P(("dp", "node", "pipe")),
            P(("dp", "node", "pipe")),
            P(("dp", "node", "pipe")),
            P(("dp", "node", "pipe"), None),
            P(("dp", "node", "pipe"), None),
            P(("dp", "node", "pipe"), None),
            P(("dp", "node", "pipe"), None),
            P(("dp", "node", "pipe")),
            P(("dp", "node", "pipe")),
        ),
        out_specs=(
            P(("dp", "node"), None),
            P(("dp", "node")),
            P(("dp", "node", "pipe"), None),
            P(("dp", "node", "pipe"), None),
            P(("dp", "node", "pipe")),
            P(("dp", "node", "pipe")),
        ),
        check_vma=False,
    )
```

time: 1320 us -> 65.9 us (0.05)
  waiting for transfers between devices: 1180 us -> 7.96 us
  blocking collectives: 102 us -> 24.6 us
  starting transfers between devices: 0.04 us -> 16.4 us
  Pallas kernels: 0 us -> 14.2 us
  between operations: 14.9 us -> 0.72 us
    reduce_scatter x1 -> x0, waiting for transfers between devices: 1180 us -> none  [shards(): lax.psum_scatter(summed[0], ('dp', 'node', 'pipe'), scatter_dimension=0,...]
    unnamed x2 -> x0, blocking collectives: 90.6 us -> none
    all_to_all x0 -> x1, blocking collectives: none -> 24.6 us  [shards(): packed = lax.all_to_all(packed, ('node', 'pipe'), 0, 0, tiled=True)]
    pallas_call x0 -> x4, Pallas kernels: none -> 14.2 us  [the longest x1 6.51 us: run_grads(): pl.pallas_call(grads_kernel, out_shape=(jax.ShapeDtypeStruct((size_xy, si...]
  transfers between devices with their start and end apart: 1 -> 6, of which waited for: 1 -> 4; matrix products, arithmetic and copies ran while one was open for 0% -> 1% of each run, Pallas kernels for 0% -> 8%
where the time goes in v2:
time: 65.9 us; the launch traced here: 65.1 us
  blocking collectives  24.6 us (37%)
  starting transfers between devices  16.4 us (25%)
  Pallas kernels  14.2 us (22%)
  waiting for transfers between devices  7.96 us (12%)
  between operations  0.72 us (1%)
  local copies, waits for them, and re-layouts  0.68 us (1%)
    all_to_all x1, blocking collectives, shards(): packed = lax.all_to_all(packed, ('node', 'pipe'), 0, 0, tiled=True)  24.6 us
    all_to_all x1, starting transfers between devices, shards(): lax.all_to_all(packed, ('dp', 'node', 'pipe'), 0, 0, tiled=True, axis_ind...  9.68 us
    pallas_call x1, Pallas kernels, run_grads(): pl.pallas_call(grads_kernel, out_shape=(jax.ShapeDtypeStruct((size_xy, si...  6.51 us
    ppermute x3, starting transfers between devices, shards(): lax.ppermute(moments, 'pipe', [(i, (i - k) % size_pipe) for i in range(si...  6 us
    pallas_call x1, Pallas kernels, run_forward(): pl.pallas_call(forward_kernel, out_shape=jax.ShapeDtypeStruct((rows, LANE...  5.26 us
    all_to_all x1, waiting for transfers between devices, shards(): lax.all_to_all(packed, ('dp', 'node', 'pipe'), 0, 0, tiled=True, axis_ind...  4.66 us
    ppermute x3, waiting for transfers between devices, shards(): lax.ppermute(moments, 'pipe', [(i, (i - k) % size_pipe) for i in range(si...  2.61 us
    pallas_call x1, Pallas kernels, run_update(): pl.pallas_call(update_kernel, out_shape=(jax.ShapeDtypeStruct((LANES, BIN...  1.61 us
  transfers between devices with their start and end apart: 6, of which 4 were waited for; matrix products, arithmetic and copies ran while one was open for 1% of the time, Pallas kernels for 8%

profile of v2, /device:TPU:2, one launch (start us, length us, event | category | flops | bytes accessed | tf_op | source)
XLA Modules:
  0.0 65.1 jit_solution(15127852188157014561)
XLA Ops:
  0.6 0.1 collective-permute-start
  0.7 5.3 %forward.1.pack = f32[384,128]{1,0:T(8,128)} custom-call(s32[1,64]{1,0:T(1,128)} %gain_exp.1, bf16[128,8192]{1,0:T(8,128)(2,1)} %hidden.3, bf16[8192,128]{1,0:T(8,128)(2,1)} %head.5, bf16[64,128]{1,0:T(8,128)(2,1)} %bitcast.12, f32[1,128]{1,0:T(1,128)} %bitcast.17, f32[1,128]{1,0:T(1,128)} %bitcast.18, s32[1,128]{1,0:T(1,128)} %bitcast.19, s32[1,8192]{1,0:T(1,128)} %row_exp.1), custom_call_target="tpu_custom_call" | custom-call | flops 268435456 | bytes 8388608 | tf_op jit(solution)/shard_map/forward/pallas_call | solution.py:124
  6.0 0.6 collective-permute-start.1
  6.6 0.6 pad_add_fusion.place
  7.2 0.7 %collective-permute-done.1.other_pack = f32[384,128]{1,0:T(8,128)S(1)} collective-permute-done((f32[384,128]{1,0:T(8,128)}, f32[384,128]{1,0:T(8,128)S(1)}, u32[]{:S(2)}, u32[]{:S(2)}) %collective-permute-start.1) | collective-permute-done | bytes 196640 | tf_op jit(solution)/shard_map/ppermute | solution.py:427
  7.9 0.0 copy-start.4
  7.9 0.0 collective-permute-done.other
  7.9 0.7 %copy-done.4 = f32[384,128]{1,0:T(8,128)} copy-done((f32[384,128]{1,0:T(8,128)}, f32[384,128]{1,0:T(8,128)S(1)}, u32[]{:S(2)}) %copy-start.4) | copy-done | bytes 196632
  8.5 6.5 %grads.1 = (bf16[16,272,128]{2,1,0:T(8,128)(2,1)}, f32[72,128]{1,0:T(8,128)}) custom-call(s32[3]{0:T(128)} %pad_add_fusion.place, bf16[128,8192]{1,0:T(8,128)(2,1)} %hidden.3, bf16[128,8192]{1,0:T(8,128)(2,1)} %collective-permute-done.other, bf16[8192,128]{1,0:T(8,128)(2,1)} %head.5, bf16[64,128]{1,0:T(8,128)(2,1)} %bitcast.13, f32[384,128]{1,0:T(8,128)} %forward.1.pack, ...), custom_call_target="tpu_custom_call" | custom-call | flops 536870912 | bytes 8388608 | tf_op jit(solution)/shard_map/grads/pallas_call | solution.py:238
  15.0 0.0 copy-start.2
  15.0 0.0 copy-start
  15.1 0.0 copy-start.1
  15.1 0.0 copy-start.3
  15.1 24.6 %all_to_all.10.parts = bf16[16,272,128]{2,1,0:T(8,128)(2,1)S(1)} all-to-all(bf16[16,272,128]{2,1,0:T(8,128)(2,1)} %get-tuple-element.14), channel_id=1, replica_groups=mesh['dp'=16,'node'=4,'pipe'=4] {'node','pipe'}, dimensions={0} | all-to-all | bytes 2228224 | tf_op jit(solution)/shard_map/all_to_all | solution.py:439
  39.7 0.9 %plane.1 = bf16[32,40,128]{2,1,0:T(8,128)(2,1)} custom-call(bf16[16,272,128]{2,1,0:T(8,128)(2,1)S(1)} %all_to_all.10.parts), custom_call_target="tpu_custom_call" | custom-call | tf_op jit(solution)/shard_map/plane/pallas_call | solution.py:288
  40.5 9.7 %all-to-all-start.1 = ((bf16[32,40,128]{2,1,0:T(8,128)(2,1)}), bf16[32,40,128]{2,1,0:T(8,128)(2,1)S(1)}, u32[]{:S(2)}, u32[]{:S(2)}) async-start(bf16[32,40,128]{2,1,0:T(8,128)(2,1)} %plane.1), calls=%async_computation.1 | async-start | bytes 655360 | tf_op jit(solution)/shard_map/all_to_all | solution.py:445
  50.2 0.0 copy-done.2
  50.2 1.9 %collective-permute-start.4 = (f32[72,128]{1,0:T(8,128)S(1)}, f32[72,128]{1,0:T(8,128)S(1)}, u32[]{:S(2)}, u32[]{:S(2)}) collective-permute-start(f32[72,128]{1,0:T(8,128)S(1)} %copy-done.2), channel_id=1, source_target_pairs={{0,1},{1,2},{2,3},{3,0},{4,5},{5,6},{6,7},{7,4},{8,9},{9,10},{10,1... | collective-permute-start | bytes 110600 | tf_op jit(solution)/shard_map/ppermute | solution.py:441
  52.1 2.7 %collective-permute-start.3 = (f32[72,128]{1,0:T(8,128)S(1)}, f32[72,128]{1,0:T(8,128)S(1)}, u32[]{:S(2)}, u32[]{:S(2)}) collective-permute-start(f32[72,128]{1,0:T(8,128)S(1)} %copy-done.2), channel_id=1, source_target_pairs={{0,2},{1,3},{2,0},{3,1},{4,6},{5,7},{6,4},{7,5},{8,10},{9,11},{10,... | collective-permute-start | bytes 110600 | tf_op jit(solution)/shard_map/ppermute | solution.py:441
  54.8 1.5 %collective-permute-start.2 = (f32[72,128]{1,0:T(8,128)S(1)}, f32[72,128]{1,0:T(8,128)S(1)}, u32[]{:S(2)}, u32[]{:S(2)}) collective-permute-start(f32[72,128]{1,0:T(8,128)S(1)} %copy-done.2), channel_id=1, source_target_pairs={{0,3},{1,0},{2,1},{3,2},{4,7},{5,4},{6,5},{7,6},{8,11},{9,8},{10,9... | collective-permute-start | bytes 110600 | tf_op jit(solution)/shard_map/ppermute | solution.py:441
  56.3 0.0 collective-permute-done.4.next_3
  56.3 1.8 %collective-permute-done.3.next_2 = f32[72,128]{1,0:T(8,128)S(1)} collective-permute-done((f32[72,128]{1,0:T(8,128)S(1)}, f32[72,128]{1,0:T(8,128)S(1)}, u32[]{:S(2)}, u32[]{:S(2)}) %collective-permute-start.3) | collective-permute-done | bytes 36896 | tf_op jit(solution)/shard_map/ppermute | solution.py:441
  58.0 0.9 %collective-permute-done.2.next_1 = f32[72,128]{1,0:T(8,128)S(1)} collective-permute-done((f32[72,128]{1,0:T(8,128)S(1)}, f32[72,128]{1,0:T(8,128)S(1)}, u32[]{:S(2)}, u32[]{:S(2)}) %collective-permute-start.2) | collective-permute-done | bytes 36896 | tf_op jit(solution)/shard_map/ppermute | solution.py:441
  58.9 4.7 %all-to-all-done.1.parts = bf16[32,40,128]{2,1,0:T(8,128)(2,1)S(1)} async-done(((bf16[32,40,128]{2,1,0:T(8,128)(2,1)}), bf16[32,40,128]{2,1,0:T(8,128)(2,1)S(1)}, u32[]{:S(2)}, u32[]{:S(2)}) %all-to-all-start.1) | async-done | bytes 327712 | tf_op jit(solution)/shard_map/all_to_all | solution.py:445
  63.5 0.0 copy-done
  63.5 0.0 copy-done.1
  63.5 0.0 copy-done.3
  63.5 1.6 %update.1 = (bf16[128,128]{1,0:T(8,128)(2,1)}, bf16[1,128]{1,0:T(2,128)(2,1)}, f32[32,128]{1,0:T(8,128)}, f32[32,128]{1,0:T(8,128)}, f32[1,32]{1,0:T(1,128)}, /*index=5*/f32[1,32]{1,0:T(1,128)}) custom-call(s32[3]{0:T(128)S(1)} %copy-done.3, bf16[32,40,128]{2,1,0:T(8,128)(2,1)S(1)} %all-to-all-done.1.parts, bf16[8192,128]{1,0:T(8,128)(2,1)S(1)} %copy-done, ...), custom_call_target="tpu_custom_call" | custom-call | tf_op jit(solution)/shard_map/update/pallas_call | solution.py:357
Async XLA Ops:
  0.6 7.2 %collective-permute-start = (bf16[128,8192]{1,0:T(8,128)(2,1)}, bf16[128,8192]{1,0:T(8,128)(2,1)}, u32[]{:S(2)}, u32[]{:S(2)}) collective-permute-start(bf16[128,8192]{1,0:T(8,128)(2,1)} %hidden.3), channel_id=1, source_target_pairs={{0,16},{16,0},{32,48},{48,32},{64,80},{80,64},{96,112},{112,96},{1... | collective-permute-start | bytes 6291464 | tf_op jit(solution)/shard_map/ppermute | solution.py:415
  6.0 1.9 %collective-permute-start.1 = (f32[384,128]{1,0:T(8,128)}, f32[384,128]{1,0:T(8,128)S(1)}, u32[]{:S(2)}, u32[]{:S(2)}) collective-permute-start(f32[384,128]{1,0:T(8,128)} %forward.1.pack), channel_id=1, source_target_pairs={{0,16},{16,0},{32,48},{48,32},{64,80},{80,64},{96,112},{112,96},{1... | collective-permute-start | bytes 589832 | tf_op jit(solution)/shard_map/ppermute | solution.py:427
  7.9 0.7 %copy-start.4 = (f32[384,128]{1,0:T(8,128)}, f32[384,128]{1,0:T(8,128)S(1)}, u32[]{:S(2)}) copy-start(f32[384,128]{1,0:T(8,128)S(1)} %collective-permute-done.1.other_pack) | copy-start | bytes 589828
  15.0 35.2 %copy-start.2 = (f32[72,128]{1,0:T(8,128)S(1)}, f32[72,128]{1,0:T(8,128)}, u32[]{:S(2)}) copy-start(f32[72,128]{1,0:T(8,128)} %get-tuple-element.15.own) | copy-start | bytes 110596
  15.0 48.5 %copy-start = (bf16[8192,128]{1,0:T(8,128)(2,1)S(1)}, bf16[8192,128]{1,0:T(8,128)(2,1)}, u32[]{:S(2)}) copy-start(bf16[8192,128]{1,0:T(8,128)(2,1)} %head.5) | copy-start | bytes 6291460
  15.1 48.5 %copy-start.1 = (bf16[8192]{0:T(1024)(128)(2,1)S(1)}, bf16[8192]{0:T(1024)(128)(2,1)}, u32[]{:S(2)}) copy-start(bf16[8192]{0:T(1024)(128)(2,1)} %param.14) | copy-start | bytes 49156
  15.1 48.5 %copy-start.3 = (s32[3]{0:T(128)S(1)}, s32[3]{0:T(128)}, u32[]{:S(2)}) copy-start(s32[3]{0:T(128)} %pad_add_fusion.place) | copy-start | bytes 40
  40.5 23.0 %all-to-all-start.1 = ((bf16[32,40,128]{2,1,0:T(8,128)(2,1)}), bf16[32,40,128]{2,1,0:T(8,128)(2,1)S(1)}, u32[]{:S(2)}, u32[]{:S(2)}) async-start(bf16[32,40,128]{2,1,0:T(8,128)(2,1)} %plane.1), calls=%async_computation.1 | async-start | bytes 655360 | tf_op jit(solution)/shard_map/all_to_all | solution.py:445
  50.2 6.0 %collective-permute-start.4 = (f32[72,128]{1,0:T(8,128)S(1)}, f32[72,128]{1,0:T(8,128)S(1)}, u32[]{:S(2)}, u32[]{:S(2)}) collective-permute-start(f32[72,128]{1,0:T(8,128)S(1)} %copy-done.2), channel_id=1, source_target_pairs={{0,1},{1,2},{2,3},{3,0},{4,5},{5,6},{6,7},{7,4},{8,9},{9,10},{10,1... | collective-permute-start | bytes 110600 | tf_op jit(solution)/shard_map/ppermute | solution.py:441
  52.1 5.9 %collective-permute-start.3 = (f32[72,128]{1,0:T(8,128)S(1)}, f32[72,128]{1,0:T(8,128)S(1)}, u32[]{:S(2)}, u32[]{:S(2)}) collective-permute-start(f32[72,128]{1,0:T(8,128)S(1)} %copy-done.2), channel_id=1, source_target_pairs={{0,2},{1,3},{2,0},{3,1},{4,6},{5,7},{6,4},{7,5},{8,10},{9,11},{10,... | collective-permute-start | bytes 110600 | tf_op jit(solution)/shard_map/ppermute | solution.py:441
  54.8 4.1 %collective-permute-start.2 = (f32[72,128]{1,0:T(8,128)S(1)}, f32[72,128]{1,0:T(8,128)S(1)}, u32[]{:S(2)}, u32[]{:S(2)}) collective-permute-start(f32[72,128]{1,0:T(8,128)S(1)} %copy-done.2), channel_id=1, source_target_pairs={{0,3},{1,0},{2,1},{3,2},{4,7},{5,4},{6,5},{7,6},{8,11},{9,8},{10,9... | collective-permute-start | bytes 110600 | tf_op jit(solution)/shard_map/ppermute | solution.py:441

commit v3 on v2

--- a/solution.py
+++ b/solution.py
@@ -25,7 +25,7 @@
 
 
 LANES = 128
-CHUNKS = 8
+CHUNKS = 4
 LIMIT_BASE = 16
 
 
@@ -56,7 +56,7 @@
 
 
 def forward_kernel(
-    gain_exp, hidden, head, gain, rewards, old_values, mask, row_exp, pack, hidden_v, head_v, sems
+    gain_exp, hidden, head, gain, rewards, old_values, mask, row_exp, pack, hidden_v, head_v, scaled_v, sems
 ):
     tokens, width = hidden.shape
     span = width // CHUNKS
@@ -91,23 +91,24 @@
     square = jnp.zeros((tokens, LANES), jnp.float32)
     for n in range(CHUNKS):
         copies[n].wait()
-        part = hidden_v[n].astype(jnp.float32)
-        part = part * part
         for m in range(span // LANES):
-            square = square + part[:, m * LANES : (m + 1) * LANES]
+            part = hidden_v[n, :, m * LANES : (m + 1) * LANES].astype(jnp.float32)
+            square = square + part * part
     inv_rms = lax.rsqrt(jnp.sum(square, axis=1, keepdims=True) / width + NORM_EPSILON)
     gains = gain[...].astype(jnp.float32)
-    logits = jnp.zeros((tokens, BINS), jnp.float32)
+    for n in range(CHUNKS):
+        first = n * span // LANES
+        for m in range(span // LANES):
+            normed = hidden_v[n, :, m * LANES : (m + 1) * LANES].astype(jnp.float32) * inv_rms
+            at = n * span + m * LANES
+            scaled_v[:, at : at + LANES] = (normed * gains[first + m : first + m + 1, :]).astype(
+                jnp.bfloat16
+            )
     for n in range(CHUNKS):
         copies[CHUNKS + n].wait()
-        first = n * span // LANES
-        gain_row = jnp.concatenate(
-            [gains[first + m : first + m + 1, :] for m in range(span // LANES)], axis=1
-        )
-        normed = hidden_v[n].astype(jnp.float32) * inv_rms
-        scaled = (normed * gain_row).astype(jnp.bfloat16)
-        logits = logits + jnp.dot(scaled, head_v[n], preferred_element_type=jnp.float32)
-    logits = LOGIT_SCALE * logits
+    logits = LOGIT_SCALE * jnp.dot(
+        scaled_v[...], head_v[...].reshape(width, BINS), preferred_element_type=jnp.float32
+    )
     shifted = jnp.exp(logits - jnp.max(logits, axis=1, keepdims=True))
     probs = shifted / jnp.sum(shifted, axis=1, keepdims=True)
     errors = (LOGIT_SCALE * counted * (probs - targets)).astype(jnp.bfloat16)
@@ -129,6 +130,7 @@
         scratch_shapes=[
             pltpu.VMEM((CHUNKS, tokens, span), jnp.bfloat16),
             pltpu.VMEM((CHUNKS, span, BINS), jnp.bfloat16),
+            pltpu.VMEM((tokens, width), jnp.bfloat16),
             pltpu.SemaphoreType.DMA((2 * CHUNKS,)),
         ],
         cost_estimate=pl.CostEstimate(
@@ -185,42 +187,50 @@
     errors = [p[:tokens, :] for p in packs]
     flipped = [e.T.astype(jnp.bfloat16) for e in errors]
     errors = [e.astype(jnp.bfloat16) for e in errors]
-    inv_rms = [jnp.concatenate([p[tokens : 2 * tokens, :]] * tiles, axis=1) for p in packs]
+    piece = 256
+    inv_rms = [jnp.concatenate([p[tokens : 2 * tokens, :]] * (piece // LANES), axis=1) for p in packs]
     blocks = width // LANES
 
     def spread(ref, first):
-        return jnp.concatenate([ref[pl.ds(first + m, 1), :] for m in range(tiles)], axis=1)
+        return jnp.concatenate(
+            [ref[pl.ds(first + m, 1), :] for m in range(piece // LANES)], axis=1
+        )
 
     for z in range(size_z):
         for copy in copies[z]:
             copy.wait()
-        first = (2 * z + side) * tiles
-        gain_row = spread(gain_f, first)
-        weight = jnp.zeros((BINS, span), jnp.float32)
-        total = jnp.zeros((1, span), jnp.float32)
-        for g in range(2):
-            normed = hidden_v[g, z].astype(jnp.float32) * inv_rms[g]
-            scaled = (normed * gain_row).astype(jnp.bfloat16)
-            back = lax.dot_general(
-                errors[g], head_v[z], (((1,), (1,)), ((), ())), preferred_element_type=jnp.float32
-            )
-            gain_part = jnp.sum(back * normed, axis=0, keepdims=True)
-            limit = spread(packs[g], 2 * tokens + blocks + first)
-            gain_q = jnp.clip(gain_part, -limit, limit).astype(jnp.bfloat16)
-            total = total + gain_q.astype(jnp.float32)
-            part = jnp.dot(flipped[g], scaled, preferred_element_type=jnp.float32)
-            limit = spread(packs[g], 2 * tokens + first)
-            weight_q = jnp.clip(part, -limit, limit).astype(jnp.bfloat16)
-            weight = weight + weight_q.astype(jnp.float32)
-        weight = weight.astype(jnp.bfloat16)
-        for m in range(tiles):
-            lanes = slice(m * LANES, (m + 1) * LANES)
-            turned = weight[:, lanes].T
-            gain_sum[m, z : z + 1, :] = total[:, lanes]
-            for n in range(LANES // rows):
-                out[m * (LANES // rows) + n, z * rows : (z + 1) * rows, :] = turned[
-                    n * rows : (n + 1) * rows, :
-                ]
+        for s in range(span // piece):
+            lanes = slice(s * piece, (s + 1) * piece)
+            first = (2 * z + side) * tiles + s * (piece // LANES)
+            gain_row = spread(gain_f, first)
+            weight = jnp.zeros((BINS, piece), jnp.float32)
+            total = jnp.zeros((1, piece), jnp.float32)
+            for g in range(2):
+                back = lax.dot_general(
+                    errors[g],
+                    head_v[z, lanes, :],
+                    (((1,), (1,)), ((), ())),
+                    preferred_element_type=jnp.float32,
+                )
+                normed = hidden_v[g, z, :, lanes].astype(jnp.float32) * inv_rms[g]
+                scaled = (normed * gain_row).astype(jnp.bfloat16)
+                part = jnp.dot(flipped[g], scaled, preferred_element_type=jnp.float32)
+                gain_part = jnp.sum(back * normed, axis=0, keepdims=True)
+                limit = spread(packs[g], 2 * tokens + blocks + first)
+                gain_q = jnp.clip(gain_part, -limit, limit).astype(jnp.bfloat16)
+                total = total + gain_q.astype(jnp.float32)
+                limit = spread(packs[g], 2 * tokens + first)
+                weight_q = jnp.clip(part, -limit, limit).astype(jnp.bfloat16)
+                weight = weight + weight_q.astype(jnp.float32)
+            weight = weight.astype(jnp.bfloat16)
+            for m in range(piece // LANES):
+                turned = weight[:, m * LANES : (m + 1) * LANES].T
+                tile = s * (piece // LANES) + m
+                gain_sum[tile, z : z + 1, :] = total[:, m * LANES : (m + 1) * LANES]
+                for n in range(LANES // rows):
+                    out[tile * (LANES // rows) + n, z * rows : (z + 1) * rows, :] = turned[
+                        n * rows : (n + 1) * rows, :
+                    ]
     for m in range(tiles):
         high = gain_sum[m].astype(jnp.bfloat16)
         low = (gain_sum[m] - high.astype(jnp.float32)).astype(jnp.bfloat16)
@@ -253,7 +263,7 @@
         cost_estimate=pl.CostEstimate(
             flops=4 * tokens * width * BINS, bytes_accessed=8 * width * tokens, transcendentals=0
         ),
-        compiler_params=pltpu.CompilerParams(vmem_limit_bytes=60 * 2**20),
+        compiler_params=pltpu.CompilerParams(vmem_limit_bytes=54579 * 2**10),
         name="grads",
     )(place, hidden, other, head, gain, *packs, *moments)
 

time: 65.9 us -> 64.8 us (0.983)
  Pallas kernels: 14.2 us -> 12.9 us
    pallas_call x1, Pallas kernels: 6.51 us -> 5.64 us  [run_grads(): pl.pallas_call(grads_kernel, out_shape=(jax.ShapeDtypeStruct((size_xy, si...]
  transfers between devices with their start and end apart: 6 -> 6, of which waited for: 4 -> 4; matrix products, arithmetic and copies ran while one was open for 1% -> 0% of each run, Pallas kernels for 8% -> 7%
where the time goes in v3:
time: 64.8 us; the launch traced here: 64.1 us
  blocking collectives  24.6 us (38%)
  starting transfers between devices  16.4 us (25%)
  Pallas kernels  12.9 us (20%)
  waiting for transfers between devices  8.49 us (13%)
  local copies, waits for them, and re-layouts  0.95 us (1%)
  between operations  0.75 us (1%)
    all_to_all x1, blocking collectives, shards(): packed = lax.all_to_all(packed, ('node', 'pipe'), 0, 0, tiled=True)  24.6 us
    all_to_all x1, starting transfers between devices, shards(): lax.all_to_all(packed, ('dp', 'node', 'pipe'), 0, 0, tiled=True, axis_ind...  9.69 us
    ppermute x3, starting transfers between devices, shards(): lax.ppermute(moments, 'pipe', [(i, (i - k) % size_pipe) for i in range(si...  6 us
    pallas_call x1, Pallas kernels, run_grads(): pl.pallas_call(grads_kernel, out_shape=(jax.ShapeDtypeStruct((size_xy, si...  5.64 us
    pallas_call x1, Pallas kernels, run_forward(): pl.pallas_call(forward_kernel, out_shape=jax.ShapeDtypeStruct((rows, LANE...  4.8 us
    all_to_all x1, waiting for transfers between devices, shards(): lax.all_to_all(packed, ('dp', 'node', 'pipe'), 0, 0, tiled=True, axis_ind...  4.67 us
    ppermute x3, waiting for transfers between devices, shards(): lax.ppermute(moments, 'pipe', [(i, (i - k) % size_pipe) for i in range(si...  2.61 us
    pallas_call x1, Pallas kernels, run_update(): pl.pallas_call(update_kernel, out_shape=(jax.ShapeDtypeStruct((LANES, BIN...  1.61 us
  transfers between devices with their start and end apart: 6, of which 4 were waited for; matrix products, arithmetic and copies ran while one was open for 0% of the time, Pallas kernels for 7%

profile of v3, /device:TPU:2, one launch (start us, length us, event | category | flops | bytes accessed | tf_op | source)
XLA Modules:
  0.0 64.1 jit_solution(15107369539612615830)
XLA Ops:
  0.6 0.1 collective-permute-start
  0.7 0.0 copy-start.2
  0.7 0.0 copy-start.3
  0.8 0.0 copy-start.4
  0.8 0.0 copy-start.5
  0.8 0.0 copy-start.6
  0.8 4.8 %forward.1.pack = f32[384,128]{1,0:T(8,128)} custom-call(s32[1,64]{1,0:T(1,128)} %gain_exp.1, bf16[128,8192]{1,0:T(8,128)(2,1)} %hidden.3, bf16[8192,128]{1,0:T(8,128)(2,1)} %head.5, bf16[64,128]{1,0:T(8,128)(2,1)} %bitcast.12, f32[1,128]{1,0:T(1,128)} %bitcast.17, f32[1,128]{1,0:T(1,128)} %bitcast.18, s32[1,128]{1,0:T(1,128)} %bitcast.19, s32[1,8192]{1,0:T(1,128)} %row_exp.1), custom_call_target="tpu_custom_call" | custom-call | flops 268435456 | bytes 8388608 | tf_op jit(solution)/shard_map/forward/pallas_call | solution.py:125
  5.6 0.6 collective-permute-start.1
  6.2 0.1 pad_add_fusion.place
  6.3 1.2 %collective-permute-done.1.other_pack = f32[384,128]{1,0:T(8,128)S(1)} collective-permute-done((f32[384,128]{1,0:T(8,128)}, f32[384,128]{1,0:T(8,128)S(1)}, u32[]{:S(2)}, u32[]{:S(2)}) %collective-permute-start.1) | collective-permute-done | bytes 196640 | tf_op jit(solution)/shard_map/ppermute | solution.py:437
  7.5 0.0 collective-permute-done.other
  7.5 0.0 copy-done.2
  7.5 0.0 copy-done.3
  7.5 0.0 copy-done.4
  7.5 0.0 copy-done.5
  7.5 0.0 copy-done.6
  7.5 0.0 copy-start.1
  7.5 0.9 %copy-done.1 = f32[384,128]{1,0:T(8,128)S(1)} copy-done((f32[384,128]{1,0:T(8,128)S(1)}, f32[384,128]{1,0:T(8,128)}, u32[]{:S(2)}) %copy-start.1) | copy-done | bytes 196632
  8.4 5.6 %grads.1 = (bf16[16,272,128]{2,1,0:T(8,128)(2,1)}, f32[72,128]{1,0:T(8,128)S(1)}) custom-call(s32[3]{0:T(128)S(1)} %pad_add_fusion.place, bf16[128,8192]{1,0:T(8,128)(2,1)} %hidden.3, bf16[128,8192]{1,0:T(8,128)(2,1)} %collective-permute-done.other, bf16[8192,128]{1,0:T(8,128)(2,1)} %head.5, bf16[64,128]{1,0:T(8,128)(2,1)S(1)} %bitcast.13, ...), custom_call_target="tpu_custom_call" | custom-call | flops 536870912 | bytes 8388608 | tf_op jit(solution)/shard_map/grads/pallas_call | solution.py:248
  14.1 0.0 copy-start
  14.1 24.6 %all_to_all.10.parts = bf16[16,272,128]{2,1,0:T(8,128)(2,1)S(1)} all-to-all(bf16[16,272,128]{2,1,0:T(8,128)(2,1)} %get-tuple-element.14), channel_id=1, replica_groups=mesh['dp'=16,'node'=4,'pipe'=4] {'node','pipe'}, dimensions={0} | all-to-all | bytes 2228224 | tf_op jit(solution)/shard_map/all_to_all | solution.py:449
  38.7 0.9 %plane.1 = bf16[32,40,128]{2,1,0:T(8,128)(2,1)} custom-call(bf16[16,272,128]{2,1,0:T(8,128)(2,1)S(1)} %all_to_all.10.parts), custom_call_target="tpu_custom_call" | custom-call | tf_op jit(solution)/shard_map/plane/pallas_call | solution.py:298
  39.5 9.7 %all-to-all-start.1 = ((bf16[32,40,128]{2,1,0:T(8,128)(2,1)}), bf16[32,40,128]{2,1,0:T(8,128)(2,1)S(1)}, u32[]{:S(2)}, u32[]{:S(2)}) async-start(bf16[32,40,128]{2,1,0:T(8,128)(2,1)} %plane.1), calls=%async_computation.1 | async-start | bytes 655360 | tf_op jit(solution)/shard_map/all_to_all | solution.py:455
  49.2 1.9 %collective-permute-start.4 = (f32[72,128]{1,0:T(8,128)S(1)}, f32[72,128]{1,0:T(8,128)S(1)}, u32[]{:S(2)}, u32[]{:S(2)}) collective-permute-start(f32[72,128]{1,0:T(8,128)S(1)} %get-tuple-element.15.own), channel_id=1, source_target_pairs={{0,1},{1,2},{2,3},{3,0},{4,5},{5,6},{6,7},{7,4},{8,9},{9,10},{10,1... | collective-permute-start | bytes 110600 | tf_op jit(solution)/shard_map/ppermute | solution.py:451
  51.1 2.7 %collective-permute-start.3 = (f32[72,128]{1,0:T(8,128)S(1)}, f32[72,128]{1,0:T(8,128)S(1)}, u32[]{:S(2)}, u32[]{:S(2)}) collective-permute-start(f32[72,128]{1,0:T(8,128)S(1)} %get-tuple-element.15.own), channel_id=1, source_target_pairs={{0,2},{1,3},{2,0},{3,1},{4,6},{5,7},{6,4},{7,5},{8,10},{9,11},{10,... | collective-permute-start | bytes 110600 | tf_op jit(solution)/shard_map/ppermute | solution.py:451
  53.8 1.5 %collective-permute-start.2 = (f32[72,128]{1,0:T(8,128)S(1)}, f32[72,128]{1,0:T(8,128)S(1)}, u32[]{:S(2)}, u32[]{:S(2)}) collective-permute-start(f32[72,128]{1,0:T(8,128)S(1)} %get-tuple-element.15.own), channel_id=1, source_target_pairs={{0,3},{1,0},{2,1},{3,2},{4,7},{5,4},{6,5},{7,6},{8,11},{9,8},{10,9... | collective-permute-start | bytes 110600 | tf_op jit(solution)/shard_map/ppermute | solution.py:451
  55.2 0.0 collective-permute-done.4.next_3
  55.2 1.6 %collective-permute-done.3.next_2 = f32[72,128]{1,0:T(8,128)S(1)} collective-permute-done((f32[72,128]{1,0:T(8,128)S(1)}, f32[72,128]{1,0:T(8,128)S(1)}, u32[]{:S(2)}, u32[]{:S(2)}) %collective-permute-start.3) | collective-permute-done | bytes 36896 | tf_op jit(solution)/shard_map/ppermute | solution.py:451
  56.9 1.0 %collective-permute-done.2.next_1 = f32[72,128]{1,0:T(8,128)S(1)} collective-permute-done((f32[72,128]{1,0:T(8,128)S(1)}, f32[72,128]{1,0:T(8,128)S(1)}, u32[]{:S(2)}, u32[]{:S(2)}) %collective-permute-start.2) | collective-permute-done | bytes 36896 | tf_op jit(solution)/shard_map/ppermute | solution.py:451
  57.9 4.7 %all-to-all-done.1.parts = bf16[32,40,128]{2,1,0:T(8,128)(2,1)S(1)} async-done(((bf16[32,40,128]{2,1,0:T(8,128)(2,1)}), bf16[32,40,128]{2,1,0:T(8,128)(2,1)S(1)}, u32[]{:S(2)}, u32[]{:S(2)}) %all-to-all-start.1) | async-done | bytes 327712 | tf_op jit(solution)/shard_map/all_to_all | solution.py:455
  62.5 0.0 copy-done
  62.5 1.6 %update.1 = (bf16[128,128]{1,0:T(8,128)(2,1)}, bf16[1,128]{1,0:T(2,128)(2,1)}, f32[32,128]{1,0:T(8,128)}, f32[32,128]{1,0:T(8,128)}, f32[1,32]{1,0:T(1,128)}, /*index=5*/f32[1,32]{1,0:T(1,128)}) custom-call(s32[3]{0:T(128)S(1)} %pad_add_fusion.place, bf16[32,40,128]{2,1,0:T(8,128)(2,1)S(1)} %all-to-all-done.1.parts, bf16[8192,128]{1,0:T(8,128)(2,1)S(1)} %copy-done, ...), custom_call_target="tpu_custom_call" | custom-call | tf_op jit(solution)/shard_map/update/pallas_call | solution.py:367
Async XLA Ops:
  0.6 6.8 %collective-permute-start = (bf16[128,8192]{1,0:T(8,128)(2,1)}, bf16[128,8192]{1,0:T(8,128)(2,1)}, u32[]{:S(2)}, u32[]{:S(2)}) collective-permute-start(bf16[128,8192]{1,0:T(8,128)(2,1)} %hidden.3), channel_id=1, source_target_pairs={{0,16},{16,0},{32,48},{48,32},{64,80},{80,64},{96,112},{112,96},{1... | collective-permute-start | bytes 6291464 | tf_op jit(solution)/shard_map/ppermute | solution.py:425
  0.7 6.7 %copy-start.2 = (bf16[8192]{0:T(1024)(128)(2,1)S(1)}, bf16[8192]{0:T(1024)(128)(2,1)}, u32[]{:S(2)}) copy-start(bf16[8192]{0:T(1024)(128)(2,1)} %param.14) | copy-start | bytes 49156
  0.7 6.7 %copy-start.3 = (f32[32,128]{1,0:T(8,128)S(1)}, f32[32,128]{1,0:T(8,128)}, u32[]{:S(2)}) copy-start(f32[32,128]{1,0:T(8,128)} %first_w.1) | copy-start | bytes 49156
  0.8 6.7 %copy-start.4 = (f32[32,128]{1,0:T(8,128)S(1)}, f32[32,128]{1,0:T(8,128)}, u32[]{:S(2)}) copy-start(f32[32,128]{1,0:T(8,128)} %second_w.1) | copy-start | bytes 49156
  0.8 6.7 %copy-start.5 = (f32[32]{0:T(128)S(1)}, f32[32]{0:T(128)}, u32[]{:S(2)}) copy-start(f32[32]{0:T(128)} %param.22) | copy-start | bytes 388
  0.8 6.7 %copy-start.6 = (f32[32]{0:T(128)S(1)}, f32[32]{0:T(128)}, u32[]{:S(2)}) copy-start(f32[32]{0:T(128)} %param.23) | copy-start | bytes 388
  5.6 1.9 %collective-permute-start.1 = (f32[384,128]{1,0:T(8,128)}, f32[384,128]{1,0:T(8,128)S(1)}, u32[]{:S(2)}, u32[]{:S(2)}) collective-permute-start(f32[384,128]{1,0:T(8,128)} %forward.1.pack), channel_id=1, source_target_pairs={{0,16},{16,0},{32,48},{48,32},{64,80},{80,64},{96,112},{112,96},{1... | collective-permute-start | bytes 589832 | tf_op jit(solution)/shard_map/ppermute | solution.py:437
  7.5 0.9 %copy-start.1 = (f32[384,128]{1,0:T(8,128)S(1)}, f32[384,128]{1,0:T(8,128)}, u32[]{:S(2)}) copy-start(f32[384,128]{1,0:T(8,128)} %forward.1.pack) | copy-start | bytes 589828
  14.1 48.4 %copy-start = (bf16[8192,128]{1,0:T(8,128)(2,1)S(1)}, bf16[8192,128]{1,0:T(8,128)(2,1)}, u32[]{:S(2)}) copy-start(bf16[8192,128]{1,0:T(8,128)(2,1)} %head.5) | copy-start | bytes 6291460
  39.5 23.0 %all-to-all-start.1 = ((bf16[32,40,128]{2,1,0:T(8,128)(2,1)}), bf16[32,40,128]{2,1,0:T(8,128)(2,1)S(1)}, u32[]{:S(2)}, u32[]{:S(2)}) async-start(bf16[32,40,128]{2,1,0:T(8,128)(2,1)} %plane.1), calls=%async_computation.1 | async-start | bytes 655360 | tf_op jit(solution)/shard_map/all_to_all | solution.py:455
  49.2 6.0 %collective-permute-start.4 = (f32[72,128]{1,0:T(8,128)S(1)}, f32[72,128]{1,0:T(8,128)S(1)}, u32[]{:S(2)}, u32[]{:S(2)}) collective-permute-start(f32[72,128]{1,0:T(8,128)S(1)} %get-tuple-element.15.own), channel_id=1, source_target_pairs={{0,1},{1,2},{2,3},{3,0},{4,5},{5,6},{6,7},{7,4},{8,9},{9,10},{10,1... | collective-permute-start | bytes 110600 | tf_op jit(solution)/shard_map/ppermute | solution.py:451
  51.1 5.7 %collective-permute-start.3 = (f32[72,128]{1,0:T(8,128)S(1)}, f32[72,128]{1,0:T(8,128)S(1)}, u32[]{:S(2)}, u32[]{:S(2)}) collective-permute-start(f32[72,128]{1,0:T(8,128)S(1)} %get-tuple-element.15.own), channel_id=1, source_target_pairs={{0,2},{1,3},{2,0},{3,1},{4,6},{5,7},{6,4},{7,5},{8,10},{9,11},{10,... | collective-permute-start | bytes 110600 | tf_op jit(solution)/shard_map/ppermute | solution.py:451
  53.8 4.1 %collective-permute-start.2 = (f32[72,128]{1,0:T(8,128)S(1)}, f32[72,128]{1,0:T(8,128)S(1)}, u32[]{:S(2)}, u32[]{:S(2)}) collective-permute-start(f32[72,128]{1,0:T(8,128)S(1)} %get-tuple-element.15.own), channel_id=1, source_target_pairs={{0,3},{1,0},{2,1},{3,2},{4,7},{5,4},{6,5},{7,6},{8,11},{9,8},{10,9... | collective-permute-start | bytes 110600 | tf_op jit(solution)/shard_map/ppermute | solution.py:451

commit v4 on v3

--- a/solution.py
+++ b/solution.py
@@ -263,7 +263,7 @@
         cost_estimate=pl.CostEstimate(
             flops=4 * tokens * width * BINS, bytes_accessed=8 * width * tokens, transcendentals=0
         ),
-        compiler_params=pltpu.CompilerParams(vmem_limit_bytes=54579 * 2**10),
+        compiler_params=pltpu.CompilerParams(vmem_limit_bytes=53248 * 2**10),
         name="grads",
     )(place, hidden, other, head, gain, *packs, *moments)
 

time: 64.8 us -> 63.6 us (0.981)
  Pallas kernels: 12.9 us -> 11.9 us
    pallas_call x1, Pallas kernels: 5.64 us -> 4.65 us  [run_grads(): pl.pallas_call(grads_kernel, out_shape=(jax.ShapeDtypeStruct((size_xy, si...]
  transfers between devices with their start and end apart: 6 -> 6, of which waited for: 4 -> 4; matrix products, arithmetic and copies ran while one was open for 0% -> 0% of each run, Pallas kernels for 7% -> 8%
where the time goes in v4:
time: 63.6 us; the launch traced here: 62.9 us
  blocking collectives  24.4 us (38%)
  starting transfers between devices  16.3 us (26%)
  Pallas kernels  11.9 us (19%)
  waiting for transfers between devices  8.49 us (13%)
  local copies, waits for them, and re-layouts  0.95 us (1%)
  between operations  0.75 us (1%)
    all_to_all x1, blocking collectives, shards(): packed = lax.all_to_all(packed, ('node', 'pipe'), 0, 0, tiled=True)  24.4 us
    all_to_all x1, starting transfers between devices, shards(): lax.all_to_all(packed, ('dp', 'node', 'pipe'), 0, 0, tiled=True, axis_ind...  9.67 us
    ppermute x3, starting transfers between devices, shards(): lax.ppermute(moments, 'pipe', [(i, (i - k) % size_pipe) for i in range(si...  6 us
    pallas_call x1, Pallas kernels, run_forward(): pl.pallas_call(forward_kernel, out_shape=jax.ShapeDtypeStruct((rows, LANE...  4.8 us
    all_to_all x1, waiting for transfers between devices, shards(): lax.all_to_all(packed, ('dp', 'node', 'pipe'), 0, 0, tiled=True, axis_ind...  4.67 us
    pallas_call x1, Pallas kernels, run_grads(): pl.pallas_call(grads_kernel, out_shape=(jax.ShapeDtypeStruct((size_xy, si...  4.65 us
    ppermute x3, waiting for transfers between devices, shards(): lax.ppermute(moments, 'pipe', [(i, (i - k) % size_pipe) for i in range(si...  2.61 us
    pallas_call x1, Pallas kernels, run_update(): pl.pallas_call(update_kernel, out_shape=(jax.ShapeDtypeStruct((LANES, BIN...  1.61 us
  transfers between devices with their start and end apart: 6, of which 4 were waited for; matrix products, arithmetic and copies ran while one was open for 0% of the time, Pallas kernels for 8%

profile of v4, /device:TPU:2, one launch (start us, length us, event | category | flops | bytes accessed | tf_op | source)
XLA Modules:
  0.0 62.9 jit_solution(2072556304562209909)
XLA Ops:
  0.6 0.1 collective-permute-start
  0.7 0.0 copy-start.2
  0.7 0.0 copy-start.3
  0.8 0.0 copy-start.4
  0.8 0.0 copy-start.5
  0.8 0.0 copy-start.6
  0.8 4.8 %forward.1.pack = f32[384,128]{1,0:T(8,128)} custom-call(s32[1,64]{1,0:T(1,128)} %gain_exp.1, bf16[128,8192]{1,0:T(8,128)(2,1)} %hidden.3, bf16[8192,128]{1,0:T(8,128)(2,1)} %head.5, bf16[64,128]{1,0:T(8,128)(2,1)} %bitcast.12, f32[1,128]{1,0:T(1,128)} %bitcast.17, f32[1,128]{1,0:T(1,128)} %bitcast.18, s32[1,128]{1,0:T(1,128)} %bitcast.19, s32[1,8192]{1,0:T(1,128)} %row_exp.1), custom_call_target="tpu_custom_call" | custom-call | flops 268435456 | bytes 8388608 | tf_op jit(solution)/shard_map/forward/pallas_call | solution.py:125
  5.6 0.6 collective-permute-start.1
  6.2 0.1 pad_add_fusion.place
  6.3 1.2 %collective-permute-done.1.other_pack = f32[384,128]{1,0:T(8,128)S(1)} collective-permute-done((f32[384,128]{1,0:T(8,128)}, f32[384,128]{1,0:T(8,128)S(1)}, u32[]{:S(2)}, u32[]{:S(2)}) %collective-permute-start.1) | collective-permute-done | bytes 196640 | tf_op jit(solution)/shard_map/ppermute | solution.py:437
  7.5 0.0 collective-permute-done.other
  7.5 0.0 copy-done.2
  7.5 0.0 copy-done.3
  7.5 0.0 copy-done.4
  7.5 0.0 copy-done.5
  7.5 0.0 copy-done.6
  7.5 0.0 copy-start.1
  7.5 0.9 %copy-done.1 = f32[384,128]{1,0:T(8,128)S(1)} copy-done((f32[384,128]{1,0:T(8,128)S(1)}, f32[384,128]{1,0:T(8,128)}, u32[]{:S(2)}) %copy-start.1) | copy-done | bytes 196632
  8.4 4.7 %grads.1 = (bf16[16,272,128]{2,1,0:T(8,128)(2,1)S(1)}, f32[72,128]{1,0:T(8,128)S(1)}) custom-call(s32[3]{0:T(128)S(1)} %pad_add_fusion.place, bf16[128,8192]{1,0:T(8,128)(2,1)} %hidden.3, bf16[128,8192]{1,0:T(8,128)(2,1)} %collective-permute-done.other, bf16[8192,128]{1,0:T(8,128)(2,1)} %head.5, bf16[64,128]{1,0:T(8,128)(2,1)S(1)} %bitcast.13, ...), custom_call_target="tpu_custom_call" | custom-call | flops 536870912 | bytes 8388608 | tf_op jit(solution)/shard_map/grads/pallas_call | solution.py:248
  13.1 0.0 copy-start
  13.1 24.4 %all_to_all.10.parts = bf16[16,272,128]{2,1,0:T(8,128)(2,1)S(1)} all-to-all(bf16[16,272,128]{2,1,0:T(8,128)(2,1)S(1)} %get-tuple-element.14), channel_id=1, replica_groups=mesh['dp'=16,'node'=4,'pipe'=4] {'node','pipe'}, dimensions={0} | all-to-all | bytes 2228224 | tf_op jit(solution)/shard_map/all_to_all | solution.py:449
  37.5 0.9 %plane.1 = bf16[32,40,128]{2,1,0:T(8,128)(2,1)} custom-call(bf16[16,272,128]{2,1,0:T(8,128)(2,1)S(1)} %all_to_all.10.parts), custom_call_target="tpu_custom_call" | custom-call | tf_op jit(solution)/shard_map/plane/pallas_call | solution.py:298
  38.4 9.7 %all-to-all-start.1 = ((bf16[32,40,128]{2,1,0:T(8,128)(2,1)}), bf16[32,40,128]{2,1,0:T(8,128)(2,1)S(1)}, u32[]{:S(2)}, u32[]{:S(2)}) async-start(bf16[32,40,128]{2,1,0:T(8,128)(2,1)} %plane.1), calls=%async_computation.1 | async-start | bytes 655360 | tf_op jit(solution)/shard_map/all_to_all | solution.py:455
  48.0 1.9 %collective-permute-start.4 = (f32[72,128]{1,0:T(8,128)S(1)}, f32[72,128]{1,0:T(8,128)S(1)}, u32[]{:S(2)}, u32[]{:S(2)}) collective-permute-start(f32[72,128]{1,0:T(8,128)S(1)} %get-tuple-element.15.own), channel_id=1, source_target_pairs={{0,1},{1,2},{2,3},{3,0},{4,5},{5,6},{6,7},{7,4},{8,9},{9,10},{10,1... | collective-permute-start | bytes 110600 | tf_op jit(solution)/shard_map/ppermute | solution.py:451
  49.9 2.7 %collective-permute-start.3 = (f32[72,128]{1,0:T(8,128)S(1)}, f32[72,128]{1,0:T(8,128)S(1)}, u32[]{:S(2)}, u32[]{:S(2)}) collective-permute-start(f32[72,128]{1,0:T(8,128)S(1)} %get-tuple-element.15.own), channel_id=1, source_target_pairs={{0,2},{1,3},{2,0},{3,1},{4,6},{5,7},{6,4},{7,5},{8,10},{9,11},{10,... | collective-permute-start | bytes 110600 | tf_op jit(solution)/shard_map/ppermute | solution.py:451
  52.6 1.5 %collective-permute-start.2 = (f32[72,128]{1,0:T(8,128)S(1)}, f32[72,128]{1,0:T(8,128)S(1)}, u32[]{:S(2)}, u32[]{:S(2)}) collective-permute-start(f32[72,128]{1,0:T(8,128)S(1)} %get-tuple-element.15.own), channel_id=1, source_target_pairs={{0,3},{1,0},{2,1},{3,2},{4,7},{5,4},{6,5},{7,6},{8,11},{9,8},{10,9... | collective-permute-start | bytes 110600 | tf_op jit(solution)/shard_map/ppermute | solution.py:451
  54.0 0.0 collective-permute-done.4.next_3
  54.0 1.8 %collective-permute-done.3.next_2 = f32[72,128]{1,0:T(8,128)S(1)} collective-permute-done((f32[72,128]{1,0:T(8,128)S(1)}, f32[72,128]{1,0:T(8,128)S(1)}, u32[]{:S(2)}, u32[]{:S(2)}) %collective-permute-start.3) | collective-permute-done | bytes 36896 | tf_op jit(solution)/shard_map/ppermute | solution.py:451
  55.8 0.9 %collective-permute-done.2.next_1 = f32[72,128]{1,0:T(8,128)S(1)} collective-permute-done((f32[72,128]{1,0:T(8,128)S(1)}, f32[72,128]{1,0:T(8,128)S(1)}, u32[]{:S(2)}, u32[]{:S(2)}) %collective-permute-start.2) | collective-permute-done | bytes 36896 | tf_op jit(solution)/shard_map/ppermute | solution.py:451
  56.6 4.7 %all-to-all-done.1.parts = bf16[32,40,128]{2,1,0:T(8,128)(2,1)S(1)} async-done(((bf16[32,40,128]{2,1,0:T(8,128)(2,1)}), bf16[32,40,128]{2,1,0:T(8,128)(2,1)S(1)}, u32[]{:S(2)}, u32[]{:S(2)}) %all-to-all-start.1) | async-done | bytes 327712 | tf_op jit(solution)/shard_map/all_to_all | solution.py:455
  61.3 0.0 copy-done
  61.3 1.6 %update.1 = (bf16[128,128]{1,0:T(8,128)(2,1)}, bf16[1,128]{1,0:T(2,128)(2,1)}, f32[32,128]{1,0:T(8,128)}, f32[32,128]{1,0:T(8,128)}, f32[1,32]{1,0:T(1,128)}, /*index=5*/f32[1,32]{1,0:T(1,128)}) custom-call(s32[3]{0:T(128)S(1)} %pad_add_fusion.place, bf16[32,40,128]{2,1,0:T(8,128)(2,1)S(1)} %all-to-all-done.1.parts, bf16[8192,128]{1,0:T(8,128)(2,1)S(1)} %copy-done, ...), custom_call_target="tpu_custom_call" | custom-call | tf_op jit(solution)/shard_map/update/pallas_call | solution.py:367
Async XLA Ops:
  0.6 6.8 %collective-permute-start = (bf16[128,8192]{1,0:T(8,128)(2,1)}, bf16[128,8192]{1,0:T(8,128)(2,1)}, u32[]{:S(2)}, u32[]{:S(2)}) collective-permute-start(bf16[128,8192]{1,0:T(8,128)(2,1)} %hidden.3), channel_id=1, source_target_pairs={{0,16},{16,0},{32,48},{48,32},{64,80},{80,64},{96,112},{112,96},{1... | collective-permute-start | bytes 6291464 | tf_op jit(solution)/shard_map/ppermute | solution.py:425
  0.7 6.7 %copy-start.2 = (bf16[8192]{0:T(1024)(128)(2,1)S(1)}, bf16[8192]{0:T(1024)(128)(2,1)}, u32[]{:S(2)}) copy-start(bf16[8192]{0:T(1024)(128)(2,1)} %param.14) | copy-start | bytes 49156
  0.7 6.7 %copy-start.3 = (f32[32,128]{1,0:T(8,128)S(1)}, f32[32,128]{1,0:T(8,128)}, u32[]{:S(2)}) copy-start(f32[32,128]{1,0:T(8,128)} %first_w.1) | copy-start | bytes 49156
  0.8 6.7 %copy-start.4 = (f32[32,128]{1,0:T(8,128)S(1)}, f32[32,128]{1,0:T(8,128)}, u32[]{:S(2)}) copy-start(f32[32,128]{1,0:T(8,128)} %second_w.1) | copy-start | bytes 49156
  0.8 6.7 %copy-start.5 = (f32[32]{0:T(128)S(1)}, f32[32]{0:T(128)}, u32[]{:S(2)}) copy-start(f32[32]{0:T(128)} %param.22) | copy-start | bytes 388
  0.8 6.7 %copy-start.6 = (f32[32]{0:T(128)S(1)}, f32[32]{0:T(128)}, u32[]{:S(2)}) copy-start(f32[32]{0:T(128)} %param.23) | copy-start | bytes 388
  5.6 1.9 %collective-permute-start.1 = (f32[384,128]{1,0:T(8,128)}, f32[384,128]{1,0:T(8,128)S(1)}, u32[]{:S(2)}, u32[]{:S(2)}) collective-permute-start(f32[384,128]{1,0:T(8,128)} %forward.1.pack), channel_id=1, source_target_pairs={{0,16},{16,0},{32,48},{48,32},{64,80},{80,64},{96,112},{112,96},{1... | collective-permute-start | bytes 589832 | tf_op jit(solution)/shard_map/ppermute | solution.py:437
  7.5 0.9 %copy-start.1 = (f32[384,128]{1,0:T(8,128)S(1)}, f32[384,128]{1,0:T(8,128)}, u32[]{:S(2)}) copy-start(f32[384,128]{1,0:T(8,128)} %forward.1.pack) | copy-start | bytes 589828
  13.1 48.2 %copy-start = (bf16[8192,128]{1,0:T(8,128)(2,1)S(1)}, bf16[8192,128]{1,0:T(8,128)(2,1)}, u32[]{:S(2)}) copy-start(bf16[8192,128]{1,0:T(8,128)(2,1)} %head.5) | copy-start | bytes 6291460
  38.4 23.0 %all-to-all-start.1 = ((bf16[32,40,128]{2,1,0:T(8,128)(2,1)}), bf16[32,40,128]{2,1,0:T(8,128)(2,1)S(1)}, u32[]{:S(2)}, u32[]{:S(2)}) async-start(bf16[32,40,128]{2,1,0:T(8,128)(2,1)} %plane.1), calls=%async_computation.1 | async-start | bytes 655360 | tf_op jit(solution)/shard_map/all_to_all | solution.py:455
  48.0 6.0 %collective-permute-start.4 = (f32[72,128]{1,0:T(8,128)S(1)}, f32[72,128]{1,0:T(8,128)S(1)}, u32[]{:S(2)}, u32[]{:S(2)}) collective-permute-start(f32[72,128]{1,0:T(8,128)S(1)} %get-tuple-element.15.own), channel_id=1, source_target_pairs={{0,1},{1,2},{2,3},{3,0},{4,5},{5,6},{6,7},{7,4},{8,9},{9,10},{10,1... | collective-permute-start | bytes 110600 | tf_op jit(solution)/shard_map/ppermute | solution.py:451
  49.9 5.9 %collective-permute-start.3 = (f32[72,128]{1,0:T(8,128)S(1)}, f32[72,128]{1,0:T(8,128)S(1)}, u32[]{:S(2)}, u32[]{:S(2)}) collective-permute-start(f32[72,128]{1,0:T(8,128)S(1)} %get-tuple-element.15.own), channel_id=1, source_target_pairs={{0,2},{1,3},{2,0},{3,1},{4,6},{5,7},{6,4},{7,5},{8,10},{9,11},{10,... | collective-permute-start | bytes 110600 | tf_op jit(solution)/shard_map/ppermute | solution.py:451
  52.6 4.1 %collective-permute-start.2 = (f32[72,128]{1,0:T(8,128)S(1)}, f32[72,128]{1,0:T(8,128)S(1)}, u32[]{:S(2)}, u32[]{:S(2)}) collective-permute-start(f32[72,128]{1,0:T(8,128)S(1)} %get-tuple-element.15.own), channel_id=1, source_target_pairs={{0,3},{1,0},{2,1},{3,2},{4,7},{5,4},{6,5},{7,6},{8,11},{9,8},{10,9... | collective-permute-start | bytes 110600 | tf_op jit(solution)/shard_map/ppermute | solution.py:451

commit v5 on v4

--- a/solution.py
+++ b/solution.py
@@ -27,6 +27,7 @@
 LANES = 128
 CHUNKS = 4
 LIMIT_BASE = 16
+KEPT_ROWS = 24576
 
 
 def limit_of(exponent):
@@ -56,7 +57,8 @@
 
 
 def forward_kernel(
-    gain_exp, hidden, head, gain, rewards, old_values, mask, row_exp, pack, hidden_v, head_v, scaled_v, sems
+    gain_exp, hidden, head, gain, rewards, old_values, mask, row_exp, sent, kept,
+    pack, hidden_v, head_v, scaled_v, sems, out_sems,
 ):
     tokens, width = hidden.shape
     span = width // CHUNKS
@@ -114,6 +116,15 @@
     errors = (LOGIT_SCALE * counted * (probs - targets)).astype(jnp.bfloat16)
     pack[:tokens, :] = errors.astype(jnp.float32)
     pack[tokens : 2 * tokens, :] = jnp.broadcast_to(inv_rms, (tokens, LANES))
+    rows = pack.shape[0]
+    results = [
+        pltpu.make_async_copy(pack, sent, out_sems.at[0]),
+        pltpu.make_async_copy(pack, kept.at[:rows, :], out_sems.at[1]),
+    ]
+    for copy in results:
+        copy.start()
+    for copy in results:
+        copy.wait()
 
 
 def run_forward(hidden, head, gain, rewards, old_values, mask, row_exp, gain_exp):
@@ -124,14 +135,19 @@
     vmem = pl.BlockSpec(memory_space=pltpu.VMEM)
     return pl.pallas_call(
         forward_kernel,
-        out_shape=jax.ShapeDtypeStruct((rows, LANES), jnp.float32),
+        out_shape=(
+            jax.ShapeDtypeStruct((rows, LANES), jnp.float32),
+            jax.ShapeDtypeStruct((KEPT_ROWS, LANES), jnp.float32),
+        ),
         in_specs=[pl.BlockSpec(memory_space=pltpu.SMEM), anywhere, anywhere] + [vmem] * 5,
-        out_specs=vmem,
+        out_specs=(anywhere, anywhere),
         scratch_shapes=[
+            pltpu.VMEM((rows, LANES), jnp.float32),
             pltpu.VMEM((CHUNKS, tokens, span), jnp.bfloat16),
             pltpu.VMEM((CHUNKS, span, BINS), jnp.bfloat16),
             pltpu.VMEM((tokens, width), jnp.bfloat16),
             pltpu.SemaphoreType.DMA((2 * CHUNKS,)),
+            pltpu.SemaphoreType.DMA((2,)),
         ],
         cost_estimate=pl.CostEstimate(
             flops=2 * tokens * width * BINS, bytes_accessed=8 * width * tokens, transcendentals=0
@@ -151,14 +167,16 @@
 
 
 def grads_kernel(
-    place, hidden, other, head, gain, pack, other_pack, first_w, second_w, first_g, second_g,
-    out, moments, hidden_v, head_v, gain_f, gain_sum, sems,
+    place, hidden, other, head, kept, gain, other_pack, first_w, second_w, first_g, second_g,
+    out, moments, hidden_v, head_v, gain_f, gain_sum, pack, sems, kept_sem,
 ):
     tokens, width = hidden.shape
     size_z, span = head_v.shape[0], head_v.shape[1]
     tiles = span // LANES
     rows = span // out.shape[0]
     side = place[0]
+    own = pltpu.make_async_copy(kept.at[: pack.shape[0], :], pack, kept_sem)
+    own.start()
     copies = []
     for z in range(size_z):
         start = pl.multiple_of((2 * z + side) * span, span)
@@ -183,6 +201,7 @@
         repeated = jnp.concatenate([values[...]] * (LANES // rows), axis=1)
         moments[2 * rows + n : 2 * rows + n + 1, :] = jnp.where(owner, repeated, 0.0)
     moments[2 * rows + 2 :, :] = jnp.zeros((6, LANES), jnp.float32)
+    own.wait()
     packs = (pack, other_pack)
     errors = [p[:tokens, :] for p in packs]
     flipped = [e.T.astype(jnp.bfloat16) for e in errors]
@@ -251,21 +270,23 @@
             jax.ShapeDtypeStruct((size_xy, size_z * rows + 2 * size_z, BINS), jnp.bfloat16),
             jax.ShapeDtypeStruct((2 * rows + 8, LANES), jnp.float32),
         ),
-        in_specs=[pl.BlockSpec(memory_space=pltpu.SMEM), anywhere, anywhere, anywhere] + [vmem] * 7,
+        in_specs=[pl.BlockSpec(memory_space=pltpu.SMEM)] + [anywhere] * 4 + [vmem] * 6,
         out_specs=(vmem, vmem),
         scratch_shapes=[
             pltpu.VMEM((2, size_z, tokens, span), jnp.bfloat16),
             pltpu.VMEM((size_z, span, BINS), jnp.bfloat16),
             pltpu.VMEM((width // LANES, LANES), jnp.float32),
             pltpu.VMEM((span // LANES, size_z, LANES), jnp.float32),
+            pltpu.VMEM(packs[1].shape, jnp.float32),
             pltpu.SemaphoreType.DMA((3, size_z)),
+            pltpu.SemaphoreType.DMA,
         ],
         cost_estimate=pl.CostEstimate(
             flops=4 * tokens * width * BINS, bytes_accessed=8 * width * tokens, transcendentals=0
         ),
         compiler_params=pltpu.CompilerParams(vmem_limit_bytes=53248 * 2**10),
         name="grads",
-    )(place, hidden, other, head, gain, *packs, *moments)
+    )(place, hidden, other, head, packs[0], gain, packs[1], *moments)
 
 
 def plane_kernel(parts, out):
@@ -424,7 +445,7 @@
 
     other_hidden = lax.ppermute(final_hidden, "dp", swap)
     gain_blocks = norm_gain.reshape(blocks, LANES)
-    pack = run_forward(
+    pack, kept = run_forward(
         final_hidden,
         value_head,
         gain_blocks,
@@ -441,7 +462,7 @@
         other_hidden,
         value_head,
         gain_blocks,
-        (pack, other_pack),
+        (kept, other_pack),
         (first_w, second_w, first_g.reshape(1, rows), second_g.reshape(1, rows)),
         size_z,
         size_xy,

time: 63.6 us -> 63.8 us (level)
  Pallas kernels: 11.9 us -> 13.1 us
  local copies, waits for them, and re-layouts: 0.95 us -> 0.03 us
    pallas_call x1, Pallas kernels: 4.65 us -> 5.66 us  [run_grads(): pl.pallas_call(grads_kernel, out_shape=(jax.ShapeDtypeStruct((size_xy, si...]
    unnamed x14 -> x12, local copies, waits for them, and re-layouts: 0.95 us -> 0.03 us
where the time goes in v5:
time: 63.8 us; the launch traced here: 63.1 us
  blocking collectives  24.4 us (38%)
  starting transfers between devices  16.3 us (26%)
  Pallas kernels  13.1 us (21%)
  waiting for transfers between devices  8.49 us (13%)
  between operations  0.74 us (1%)
    all_to_all x1, blocking collectives, shards(): packed = lax.all_to_all(packed, ('node', 'pipe'), 0, 0, tiled=True)  24.4 us
    all_to_all x1, starting transfers between devices, shards(): lax.all_to_all(packed, ('dp', 'node', 'pipe'), 0, 0, tiled=True, axis_ind...  9.67 us
    ppermute x3, starting transfers between devices, shards(): lax.ppermute(moments, 'pipe', [(i, (i - k) % size_pipe) for i in range(si...  6 us
    pallas_call x1, Pallas kernels, run_grads(): pl.pallas_call(grads_kernel, out_shape=(jax.ShapeDtypeStruct((size_xy, si...  5.66 us
    pallas_call x1, Pallas kernels, run_forward(): pl.pallas_call(forward_kernel, out_shape=(jax.ShapeDtypeStruct((rows, LAN...  4.92 us
    all_to_all x1, waiting for transfers between devices, shards(): lax.all_to_all(packed, ('dp', 'node', 'pipe'), 0, 0, tiled=True, axis_ind...  4.67 us
    ppermute x3, waiting for transfers between devices, shards(): lax.ppermute(moments, 'pipe', [(i, (i - k) % size_pipe) for i in range(si...  2.61 us
    pallas_call x1, Pallas kernels, run_update(): pl.pallas_call(update_kernel, out_shape=(jax.ShapeDtypeStruct((LANES, BIN...  1.61 us
  transfers between devices with their start and end apart: 6, of which 4 were waited for; matrix products, arithmetic and copies ran while one was open for 0% of the time, Pallas kernels for 8%

profile of v5, /device:TPU:2, one launch (start us, length us, event | category | flops | bytes accessed | tf_op | source)
XLA Modules:
  0.0 63.1 jit_solution(18121852273982639654)
XLA Ops:
  0.6 0.1 collective-permute-start
  0.7 0.0 copy-start.1
  0.7 0.0 copy-start.2
  0.8 0.0 copy-start.3
  0.8 0.0 copy-start.4
  0.8 0.0 copy-start.5
  0.8 4.9 %forward.1 = (f32[384,128]{1,0:T(8,128)}, f32[24576,128]{1,0:T(8,128)}) custom-call(s32[1,64]{1,0:T(1,128)} %gain_exp.1, bf16[128,8192]{1,0:T(8,128)(2,1)} %hidden.3, bf16[8192,128]{1,0:T(8,128)(2,1)} %head.5, bf16[64,128]{1,0:T(8,128)(2,1)} %bitcast.12, f32[1,128]{1,0:T(1,128)} %bitcast.17, f32[1,128]{1,0:T(1,128)} %bitcast.18, s32[1,128]{1,0:T(1,128)} %bitcast.19, ...), custom_call_target="tpu_custom_call" | custom-call | flops 268435456 | bytes 8388608 | tf_op jit(solution)/shard_map/forward/pallas_call | solution.py:136
  5.7 0.6 collective-permute-start.1
  6.3 0.1 pad_add_fusion.place
  6.4 1.2 %collective-permute-done.1.other_pack = f32[384,128]{1,0:T(8,128)S(1)} collective-permute-done((f32[384,128]{1,0:T(8,128)}, f32[384,128]{1,0:T(8,128)S(1)}, u32[]{:S(2)}, u32[]{:S(2)}) %collective-permute-start.1) | collective-permute-done | bytes 196640 | tf_op jit(solution)/shard_map/ppermute | solution.py:458
  7.6 0.0 collective-permute-done.other
  7.6 0.0 copy-done.1
  7.6 0.0 copy-done.2
  7.6 0.0 copy-done.3
  7.6 0.0 copy-done.4
  7.6 0.0 copy-done.5
  7.6 5.7 %grads.1 = (bf16[16,272,128]{2,1,0:T(8,128)(2,1)S(1)}, f32[72,128]{1,0:T(8,128)S(1)}) custom-call(s32[3]{0:T(128)S(1)} %pad_add_fusion.place, bf16[128,8192]{1,0:T(8,128)(2,1)} %hidden.3, bf16[128,8192]{1,0:T(8,128)(2,1)} %collective-permute-done.other, bf16[8192,128]{1,0:T(8,128)(2,1)} %head.5, f32[24576,128]{1,0:T(8,128)} %get-tuple-element.16.kept, ...), custom_call_target="tpu_custom_call" | custom-call | flops 536870912 | bytes 8388608 | tf_op jit(solution)/shard_map/grads/pallas_call | solution.py:267
  13.3 0.0 copy-start
  13.3 24.4 %all_to_all.10.parts = bf16[16,272,128]{2,1,0:T(8,128)(2,1)S(1)} all-to-all(bf16[16,272,128]{2,1,0:T(8,128)(2,1)S(1)} %get-tuple-element.18), channel_id=1, replica_groups=mesh['dp'=16,'node'=4,'pipe'=4] {'node','pipe'}, dimensions={0} | all-to-all | bytes 2228224 | tf_op jit(solution)/shard_map/all_to_all | solution.py:470
  37.7 0.9 %plane.1 = bf16[32,40,128]{2,1,0:T(8,128)(2,1)} custom-call(bf16[16,272,128]{2,1,0:T(8,128)(2,1)S(1)} %all_to_all.10.parts), custom_call_target="tpu_custom_call" | custom-call | tf_op jit(solution)/shard_map/plane/pallas_call | solution.py:319
  38.6 9.7 %all-to-all-start.1 = ((bf16[32,40,128]{2,1,0:T(8,128)(2,1)}), bf16[32,40,128]{2,1,0:T(8,128)(2,1)S(1)}, u32[]{:S(2)}, u32[]{:S(2)}) async-start(bf16[32,40,128]{2,1,0:T(8,128)(2,1)} %plane.1), calls=%async_computation.1 | async-start | bytes 655360 | tf_op jit(solution)/shard_map/all_to_all | solution.py:476
  48.2 1.9 %collective-permute-start.4 = (f32[72,128]{1,0:T(8,128)S(1)}, f32[72,128]{1,0:T(8,128)S(1)}, u32[]{:S(2)}, u32[]{:S(2)}) collective-permute-start(f32[72,128]{1,0:T(8,128)S(1)} %get-tuple-element.19.own), channel_id=1, source_target_pairs={{0,1},{1,2},{2,3},{3,0},{4,5},{5,6},{6,7},{7,4},{8,9},{9,10},{10,1... | collective-permute-start | bytes 110600 | tf_op jit(solution)/shard_map/ppermute | solution.py:472
  50.1 2.7 %collective-permute-start.3 = (f32[72,128]{1,0:T(8,128)S(1)}, f32[72,128]{1,0:T(8,128)S(1)}, u32[]{:S(2)}, u32[]{:S(2)}) collective-permute-start(f32[72,128]{1,0:T(8,128)S(1)} %get-tuple-element.19.own), channel_id=1, source_target_pairs={{0,2},{1,3},{2,0},{3,1},{4,6},{5,7},{6,4},{7,5},{8,10},{9,11},{10,... | collective-permute-start | bytes 110600 | tf_op jit(solution)/shard_map/ppermute | solution.py:472
  52.8 1.5 %collective-permute-start.2 = (f32[72,128]{1,0:T(8,128)S(1)}, f32[72,128]{1,0:T(8,128)S(1)}, u32[]{:S(2)}, u32[]{:S(2)}) collective-permute-start(f32[72,128]{1,0:T(8,128)S(1)} %get-tuple-element.19.own), channel_id=1, source_target_pairs={{0,3},{1,0},{2,1},{3,2},{4,7},{5,4},{6,5},{7,6},{8,11},{9,8},{10,9... | collective-permute-start | bytes 110600 | tf_op jit(solution)/shard_map/ppermute | solution.py:472
  54.2 0.0 collective-permute-done.4.next_3
  54.2 1.8 %collective-permute-done.3.next_2 = f32[72,128]{1,0:T(8,128)S(1)} collective-permute-done((f32[72,128]{1,0:T(8,128)S(1)}, f32[72,128]{1,0:T(8,128)S(1)}, u32[]{:S(2)}, u32[]{:S(2)}) %collective-permute-start.3) | collective-permute-done | bytes 36896 | tf_op jit(solution)/shard_map/ppermute | solution.py:472
  56.0 0.9 %collective-permute-done.2.next_1 = f32[72,128]{1,0:T(8,128)S(1)} collective-permute-done((f32[72,128]{1,0:T(8,128)S(1)}, f32[72,128]{1,0:T(8,128)S(1)}, u32[]{:S(2)}, u32[]{:S(2)}) %collective-permute-start.2) | collective-permute-done | bytes 36896 | tf_op jit(solution)/shard_map/ppermute | solution.py:472
  56.8 4.7 %all-to-all-done.1.parts = bf16[32,40,128]{2,1,0:T(8,128)(2,1)S(1)} async-done(((bf16[32,40,128]{2,1,0:T(8,128)(2,1)}), bf16[32,40,128]{2,1,0:T(8,128)(2,1)S(1)}, u32[]{:S(2)}, u32[]{:S(2)}) %all-to-all-start.1) | async-done | bytes 327712 | tf_op jit(solution)/shard_map/all_to_all | solution.py:476
  61.5 0.0 copy-done
  61.5 1.6 %update.1 = (bf16[128,128]{1,0:T(8,128)(2,1)}, bf16[1,128]{1,0:T(2,128)(2,1)}, f32[32,128]{1,0:T(8,128)}, f32[32,128]{1,0:T(8,128)}, f32[1,32]{1,0:T(1,128)}, /*index=5*/f32[1,32]{1,0:T(1,128)}) custom-call(s32[3]{0:T(128)S(1)} %pad_add_fusion.place, bf16[32,40,128]{2,1,0:T(8,128)(2,1)S(1)} %all-to-all-done.1.parts, bf16[8192,128]{1,0:T(8,128)(2,1)S(1)} %copy-done, ...), custom_call_target="tpu_custom_call" | custom-call | tf_op jit(solution)/shard_map/update/pallas_call | solution.py:388
Async XLA Ops:
  0.6 6.9 %collective-permute-start = (bf16[128,8192]{1,0:T(8,128)(2,1)}, bf16[128,8192]{1,0:T(8,128)(2,1)}, u32[]{:S(2)}, u32[]{:S(2)}) collective-permute-start(bf16[128,8192]{1,0:T(8,128)(2,1)} %hidden.3), channel_id=1, source_target_pairs={{0,16},{16,0},{32,48},{48,32},{64,80},{80,64},{96,112},{112,96},{1... | collective-permute-start | bytes 6291464 | tf_op jit(solution)/shard_map/ppermute | solution.py:446
  0.7 6.8 %copy-start.1 = (bf16[8192]{0:T(1024)(128)(2,1)S(1)}, bf16[8192]{0:T(1024)(128)(2,1)}, u32[]{:S(2)}) copy-start(bf16[8192]{0:T(1024)(128)(2,1)} %param.14) | copy-start | bytes 49156
  0.7 6.8 %copy-start.2 = (f32[32,128]{1,0:T(8,128)S(1)}, f32[32,128]{1,0:T(8,128)}, u32[]{:S(2)}) copy-start(f32[32,128]{1,0:T(8,128)} %first_w.1) | copy-start | bytes 49156
  0.8 6.8 %copy-start.3 = (f32[32,128]{1,0:T(8,128)S(1)}, f32[32,128]{1,0:T(8,128)}, u32[]{:S(2)}) copy-start(f32[32,128]{1,0:T(8,128)} %second_w.1) | copy-start | bytes 49156
  0.8 6.8 %copy-start.4 = (f32[32]{0:T(128)S(1)}, f32[32]{0:T(128)}, u32[]{:S(2)}) copy-start(f32[32]{0:T(128)} %param.22) | copy-start | bytes 388
  0.8 6.8 %copy-start.5 = (f32[32]{0:T(128)S(1)}, f32[32]{0:T(128)}, u32[]{:S(2)}) copy-start(f32[32]{0:T(128)} %param.23) | copy-start | bytes 388
  5.7 1.9 %collective-permute-start.1 = (f32[384,128]{1,0:T(8,128)}, f32[384,128]{1,0:T(8,128)S(1)}, u32[]{:S(2)}, u32[]{:S(2)}) collective-permute-start(f32[384,128]{1,0:T(8,128)} %get-tuple-element.17), channel_id=1, source_target_pairs={{0,16},{16,0},{32,48},{48,32},{64,80},{80,64},{96,112},{112,96},{1... | collective-permute-start | bytes 589832 | tf_op jit(solution)/shard_map/ppermute | solution.py:458
  13.3 48.2 %copy-start = (bf16[8192,128]{1,0:T(8,128)(2,1)S(1)}, bf16[8192,128]{1,0:T(8,128)(2,1)}, u32[]{:S(2)}) copy-start(bf16[8192,128]{1,0:T(8,128)(2,1)} %head.5) | copy-start | bytes 6291460
  38.6 23.0 %all-to-all-start.1 = ((bf16[32,40,128]{2,1,0:T(8,128)(2,1)}), bf16[32,40,128]{2,1,0:T(8,128)(2,1)S(1)}, u32[]{:S(2)}, u32[]{:S(2)}) async-start(bf16[32,40,128]{2,1,0:T(8,128)(2,1)} %plane.1), calls=%async_computation.1 | async-start | bytes 655360 | tf_op jit(solution)/shard_map/all_to_all | solution.py:476
  48.2 6.0 %collective-permute-start.4 = (f32[72,128]{1,0:T(8,128)S(1)}, f32[72,128]{1,0:T(8,128)S(1)}, u32[]{:S(2)}, u32[]{:S(2)}) collective-permute-start(f32[72,128]{1,0:T(8,128)S(1)} %get-tuple-element.19.own), channel_id=1, source_target_pairs={{0,1},{1,2},{2,3},{3,0},{4,5},{5,6},{6,7},{7,4},{8,9},{9,10},{10,1... | collective-permute-start | bytes 110600 | tf_op jit(solution)/shard_map/ppermute | solution.py:472
  50.1 5.9 %collective-permute-start.3 = (f32[72,128]{1,0:T(8,128)S(1)}, f32[72,128]{1,0:T(8,128)S(1)}, u32[]{:S(2)}, u32[]{:S(2)}) collective-permute-start(f32[72,128]{1,0:T(8,128)S(1)} %get-tuple-element.19.own), channel_id=1, source_target_pairs={{0,2},{1,3},{2,0},{3,1},{4,6},{5,7},{6,4},{7,5},{8,10},{9,11},{10,... | collective-permute-start | bytes 110600 | tf_op jit(solution)/shard_map/ppermute | solution.py:472
  52.8 4.1 %collective-permute-start.2 = (f32[72,128]{1,0:T(8,128)S(1)}, f32[72,128]{1,0:T(8,128)S(1)}, u32[]{:S(2)}, u32[]{:S(2)}) collective-permute-start(f32[72,128]{1,0:T(8,128)S(1)} %get-tuple-element.19.own), channel_id=1, source_target_pairs={{0,3},{1,0},{2,1},{3,2},{4,7},{5,4},{6,5},{7,6},{8,11},{9,8},{10,9... | collective-permute-start | bytes 110600 | tf_op jit(solution)/shard_map/ppermute | solution.py:472

commit v6 on v5

--- a/solution.py
+++ b/solution.py
@@ -201,13 +201,19 @@
         repeated = jnp.concatenate([values[...]] * (LANES // rows), axis=1)
         moments[2 * rows + n : 2 * rows + n + 1, :] = jnp.where(owner, repeated, 0.0)
     moments[2 * rows + 2 :, :] = jnp.zeros((6, LANES), jnp.float32)
-    own.wait()
     packs = (pack, other_pack)
-    errors = [p[:tokens, :] for p in packs]
-    flipped = [e.T.astype(jnp.bfloat16) for e in errors]
-    errors = [e.astype(jnp.bfloat16) for e in errors]
     piece = 256
-    inv_rms = [jnp.concatenate([p[tokens : 2 * tokens, :]] * (piece // LANES), axis=1) for p in packs]
+    errors, flipped, inv_rms = {}, {}, {}
+
+    def prepare(g):
+        values = packs[g][:tokens, :]
+        flipped[g] = values.T.astype(jnp.bfloat16)
+        errors[g] = values.astype(jnp.bfloat16)
+        inv_rms[g] = jnp.concatenate(
+            [packs[g][tokens : 2 * tokens, :]] * (piece // LANES), axis=1
+        )
+
+    prepare(1)
     blocks = width // LANES
 
     def spread(ref, first):
@@ -224,7 +230,10 @@
             gain_row = spread(gain_f, first)
             weight = jnp.zeros((BINS, piece), jnp.float32)
             total = jnp.zeros((1, piece), jnp.float32)
-            for g in range(2):
+            for g in (1, 0):
+                if g not in errors:
+                    own.wait()
+                    prepare(g)
                 back = lax.dot_general(
                     errors[g],
                     head_v[z, lanes, :],

time: 63.8 us -> 63.6 us (level)
  no operation moved by 1% of the time
where the time goes in v6:
time: 63.6 us; the launch traced here: 63 us
  blocking collectives  24.4 us (38%)
  starting transfers between devices  16.4 us (26%)
  Pallas kernels  12.9 us (20%)
  waiting for transfers between devices  8.49 us (13%)
  between operations  0.74 us (1%)
    all_to_all x1, blocking collectives, shards(): packed = lax.all_to_all(packed, ('node', 'pipe'), 0, 0, tiled=True)  24.4 us
    all_to_all x1, starting transfers between devices, shards(): lax.all_to_all(packed, ('dp', 'node', 'pipe'), 0, 0, tiled=True, axis_ind...  9.67 us
    ppermute x3, starting transfers between devices, shards(): lax.ppermute(moments, 'pipe', [(i, (i - k) % size_pipe) for i in range(si...  6 us
    pallas_call x1, Pallas kernels, run_grads(): pl.pallas_call(grads_kernel, out_shape=(jax.ShapeDtypeStruct((size_xy, si...  5.5 us
    pallas_call x1, Pallas kernels, run_forward(): pl.pallas_call(forward_kernel, out_shape=(jax.ShapeDtypeStruct((rows, LAN...  4.92 us
    all_to_all x1, waiting for transfers between devices, shards(): lax.all_to_all(packed, ('dp', 'node', 'pipe'), 0, 0, tiled=True, axis_ind...  4.67 us
    ppermute x3, waiting for transfers between devices, shards(): lax.ppermute(moments, 'pipe', [(i, (i - k) % size_pipe) for i in range(si...  2.61 us
    pallas_call x1, Pallas kernels, run_update(): pl.pallas_call(update_kernel, out_shape=(jax.ShapeDtypeStruct((LANES, BIN...  1.61 us
  transfers between devices with their start and end apart: 6, of which 4 were waited for; matrix products, arithmetic and copies ran while one was open for 0% of the time, Pallas kernels for 8%

profile of v6, /device:TPU:2, one launch (start us, length us, event | category | flops | bytes accessed | tf_op | source)
XLA Modules:
  0.0 63.0 jit_solution(8374380831323161058)
XLA Ops:
  0.6 0.1 collective-permute-start
  0.7 0.0 copy-start.1
  0.7 0.0 copy-start.2
  0.8 0.0 copy-start.3
  0.8 0.0 copy-start.4
  0.8 0.0 copy-start.5
  0.8 4.9 %forward.1 = (f32[384,128]{1,0:T(8,128)}, f32[24576,128]{1,0:T(8,128)}) custom-call(s32[1,64]{1,0:T(1,128)} %gain_exp.1, bf16[128,8192]{1,0:T(8,128)(2,1)} %hidden.3, bf16[8192,128]{1,0:T(8,128)(2,1)} %head.5, bf16[64,128]{1,0:T(8,128)(2,1)} %bitcast.12, f32[1,128]{1,0:T(1,128)} %bitcast.17, f32[1,128]{1,0:T(1,128)} %bitcast.18, s32[1,128]{1,0:T(1,128)} %bitcast.19, ...), custom_call_target="tpu_custom_call" | custom-call | flops 268435456 | bytes 8388608 | tf_op jit(solution)/shard_map/forward/pallas_call | solution.py:136
  5.7 0.6 collective-permute-start.1
  6.3 0.1 pad_add_fusion.place
  6.4 1.2 %collective-permute-done.1.other_pack = f32[384,128]{1,0:T(8,128)S(1)} collective-permute-done((f32[384,128]{1,0:T(8,128)}, f32[384,128]{1,0:T(8,128)S(1)}, u32[]{:S(2)}, u32[]{:S(2)}) %collective-permute-start.1) | collective-permute-done | bytes 196640 | tf_op jit(solution)/shard_map/ppermute | solution.py:467
  7.6 0.0 collective-permute-done.other
  7.6 0.0 copy-done.1
  7.6 0.0 copy-done.2
  7.6 0.0 copy-done.3
  7.6 0.0 copy-done.4
  7.6 0.0 copy-done.5
  7.6 5.5 %grads.1 = (bf16[16,272,128]{2,1,0:T(8,128)(2,1)S(1)}, f32[72,128]{1,0:T(8,128)S(1)}) custom-call(s32[3]{0:T(128)S(1)} %pad_add_fusion.place, bf16[128,8192]{1,0:T(8,128)(2,1)} %hidden.3, bf16[128,8192]{1,0:T(8,128)(2,1)} %collective-permute-done.other, bf16[8192,128]{1,0:T(8,128)(2,1)} %head.5, f32[24576,128]{1,0:T(8,128)} %get-tuple-element.16.kept, ...), custom_call_target="tpu_custom_call" | custom-call | flops 536870912 | bytes 8388608 | tf_op jit(solution)/shard_map/grads/pallas_call | solution.py:276
  13.1 0.0 copy-start
  13.1 24.4 %all_to_all.10.parts = bf16[16,272,128]{2,1,0:T(8,128)(2,1)S(1)} all-to-all(bf16[16,272,128]{2,1,0:T(8,128)(2,1)S(1)} %get-tuple-element.18), channel_id=1, replica_groups=mesh['dp'=16,'node'=4,'pipe'=4] {'node','pipe'}, dimensions={0} | all-to-all | bytes 2228224 | tf_op jit(solution)/shard_map/all_to_all | solution.py:479
  37.5 0.9 %plane.1 = bf16[32,40,128]{2,1,0:T(8,128)(2,1)} custom-call(bf16[16,272,128]{2,1,0:T(8,128)(2,1)S(1)} %all_to_all.10.parts), custom_call_target="tpu_custom_call" | custom-call | tf_op jit(solution)/shard_map/plane/pallas_call | solution.py:328
  38.4 9.7 %all-to-all-start.1 = ((bf16[32,40,128]{2,1,0:T(8,128)(2,1)}), bf16[32,40,128]{2,1,0:T(8,128)(2,1)S(1)}, u32[]{:S(2)}, u32[]{:S(2)}) async-start(bf16[32,40,128]{2,1,0:T(8,128)(2,1)} %plane.1), calls=%async_computation.1 | async-start | bytes 655360 | tf_op jit(solution)/shard_map/all_to_all | solution.py:485
  48.1 1.9 %collective-permute-start.4 = (f32[72,128]{1,0:T(8,128)S(1)}, f32[72,128]{1,0:T(8,128)S(1)}, u32[]{:S(2)}, u32[]{:S(2)}) collective-permute-start(f32[72,128]{1,0:T(8,128)S(1)} %get-tuple-element.19.own), channel_id=1, source_target_pairs={{0,1},{1,2},{2,3},{3,0},{4,5},{5,6},{6,7},{7,4},{8,9},{9,10},{10,1... | collective-permute-start | bytes 110600 | tf_op jit(solution)/shard_map/ppermute | solution.py:481
  49.9 2.7 %collective-permute-start.3 = (f32[72,128]{1,0:T(8,128)S(1)}, f32[72,128]{1,0:T(8,128)S(1)}, u32[]{:S(2)}, u32[]{:S(2)}) collective-permute-start(f32[72,128]{1,0:T(8,128)S(1)} %get-tuple-element.19.own), channel_id=1, source_target_pairs={{0,2},{1,3},{2,0},{3,1},{4,6},{5,7},{6,4},{7,5},{8,10},{9,11},{10,... | collective-permute-start | bytes 110600 | tf_op jit(solution)/shard_map/ppermute | solution.py:481
  52.6 1.5 %collective-permute-start.2 = (f32[72,128]{1,0:T(8,128)S(1)}, f32[72,128]{1,0:T(8,128)S(1)}, u32[]{:S(2)}, u32[]{:S(2)}) collective-permute-start(f32[72,128]{1,0:T(8,128)S(1)} %get-tuple-element.19.own), channel_id=1, source_target_pairs={{0,3},{1,0},{2,1},{3,2},{4,7},{5,4},{6,5},{7,6},{8,11},{9,8},{10,9... | collective-permute-start | bytes 110600 | tf_op jit(solution)/shard_map/ppermute | solution.py:481
  54.1 0.0 collective-permute-done.4.next_3
  54.1 1.8 %collective-permute-done.3.next_2 = f32[72,128]{1,0:T(8,128)S(1)} collective-permute-done((f32[72,128]{1,0:T(8,128)S(1)}, f32[72,128]{1,0:T(8,128)S(1)}, u32[]{:S(2)}, u32[]{:S(2)}) %collective-permute-start.3) | collective-permute-done | bytes 36896 | tf_op jit(solution)/shard_map/ppermute | solution.py:481
  55.8 0.9 %collective-permute-done.2.next_1 = f32[72,128]{1,0:T(8,128)S(1)} collective-permute-done((f32[72,128]{1,0:T(8,128)S(1)}, f32[72,128]{1,0:T(8,128)S(1)}, u32[]{:S(2)}, u32[]{:S(2)}) %collective-permute-start.2) | collective-permute-done | bytes 36896 | tf_op jit(solution)/shard_map/ppermute | solution.py:481
  56.7 4.7 %all-to-all-done.1.parts = bf16[32,40,128]{2,1,0:T(8,128)(2,1)S(1)} async-done(((bf16[32,40,128]{2,1,0:T(8,128)(2,1)}), bf16[32,40,128]{2,1,0:T(8,128)(2,1)S(1)}, u32[]{:S(2)}, u32[]{:S(2)}) %all-to-all-start.1) | async-done | bytes 327712 | tf_op jit(solution)/shard_map/all_to_all | solution.py:485
  61.3 0.0 copy-done
  61.4 1.6 %update.1 = (bf16[128,128]{1,0:T(8,128)(2,1)}, bf16[1,128]{1,0:T(2,128)(2,1)}, f32[32,128]{1,0:T(8,128)}, f32[32,128]{1,0:T(8,128)}, f32[1,32]{1,0:T(1,128)}, /*index=5*/f32[1,32]{1,0:T(1,128)}) custom-call(s32[3]{0:T(128)S(1)} %pad_add_fusion.place, bf16[32,40,128]{2,1,0:T(8,128)(2,1)S(1)} %all-to-all-done.1.parts, bf16[8192,128]{1,0:T(8,128)(2,1)S(1)} %copy-done, ...), custom_call_target="tpu_custom_call" | custom-call | tf_op jit(solution)/shard_map/update/pallas_call | solution.py:397
Async XLA Ops:
  0.6 6.9 %collective-permute-start = (bf16[128,8192]{1,0:T(8,128)(2,1)}, bf16[128,8192]{1,0:T(8,128)(2,1)}, u32[]{:S(2)}, u32[]{:S(2)}) collective-permute-start(bf16[128,8192]{1,0:T(8,128)(2,1)} %hidden.3), channel_id=1, source_target_pairs={{0,16},{16,0},{32,48},{48,32},{64,80},{80,64},{96,112},{112,96},{1... | collective-permute-start | bytes 6291464 | tf_op jit(solution)/shard_map/ppermute | solution.py:455
  0.7 6.8 %copy-start.1 = (bf16[8192]{0:T(1024)(128)(2,1)S(1)}, bf16[8192]{0:T(1024)(128)(2,1)}, u32[]{:S(2)}) copy-start(bf16[8192]{0:T(1024)(128)(2,1)} %param.14) | copy-start | bytes 49156
  0.7 6.8 %copy-start.2 = (f32[32,128]{1,0:T(8,128)S(1)}, f32[32,128]{1,0:T(8,128)}, u32[]{:S(2)}) copy-start(f32[32,128]{1,0:T(8,128)} %first_w.1) | copy-start | bytes 49156
  0.8 6.8 %copy-start.3 = (f32[32,128]{1,0:T(8,128)S(1)}, f32[32,128]{1,0:T(8,128)}, u32[]{:S(2)}) copy-start(f32[32,128]{1,0:T(8,128)} %second_w.1) | copy-start | bytes 49156
  0.8 6.8 %copy-start.4 = (f32[32]{0:T(128)S(1)}, f32[32]{0:T(128)}, u32[]{:S(2)}) copy-start(f32[32]{0:T(128)} %param.22) | copy-start | bytes 388
  0.8 6.8 %copy-start.5 = (f32[32]{0:T(128)S(1)}, f32[32]{0:T(128)}, u32[]{:S(2)}) copy-start(f32[32]{0:T(128)} %param.23) | copy-start | bytes 388
  5.7 1.9 %collective-permute-start.1 = (f32[384,128]{1,0:T(8,128)}, f32[384,128]{1,0:T(8,128)S(1)}, u32[]{:S(2)}, u32[]{:S(2)}) collective-permute-start(f32[384,128]{1,0:T(8,128)} %get-tuple-element.17), channel_id=1, source_target_pairs={{0,16},{16,0},{32,48},{48,32},{64,80},{80,64},{96,112},{112,96},{1... | collective-permute-start | bytes 589832 | tf_op jit(solution)/shard_map/ppermute | solution.py:467
  13.1 48.2 %copy-start = (bf16[8192,128]{1,0:T(8,128)(2,1)S(1)}, bf16[8192,128]{1,0:T(8,128)(2,1)}, u32[]{:S(2)}) copy-start(bf16[8192,128]{1,0:T(8,128)(2,1)} %head.5) | copy-start | bytes 6291460
  38.4 23.0 %all-to-all-start.1 = ((bf16[32,40,128]{2,1,0:T(8,128)(2,1)}), bf16[32,40,128]{2,1,0:T(8,128)(2,1)S(1)}, u32[]{:S(2)}, u32[]{:S(2)}) async-start(bf16[32,40,128]{2,1,0:T(8,128)(2,1)} %plane.1), calls=%async_computation.1 | async-start | bytes 655360 | tf_op jit(solution)/shard_map/all_to_all | solution.py:485
  48.1 6.0 %collective-permute-start.4 = (f32[72,128]{1,0:T(8,128)S(1)}, f32[72,128]{1,0:T(8,128)S(1)}, u32[]{:S(2)}, u32[]{:S(2)}) collective-permute-start(f32[72,128]{1,0:T(8,128)S(1)} %get-tuple-element.19.own), channel_id=1, source_target_pairs={{0,1},{1,2},{2,3},{3,0},{4,5},{5,6},{6,7},{7,4},{8,9},{9,10},{10,1... | collective-permute-start | bytes 110600 | tf_op jit(solution)/shard_map/ppermute | solution.py:481
  49.9 5.9 %collective-permute-start.3 = (f32[72,128]{1,0:T(8,128)S(1)}, f32[72,128]{1,0:T(8,128)S(1)}, u32[]{:S(2)}, u32[]{:S(2)}) collective-permute-start(f32[72,128]{1,0:T(8,128)S(1)} %get-tuple-element.19.own), channel_id=1, source_target_pairs={{0,2},{1,3},{2,0},{3,1},{4,6},{5,7},{6,4},{7,5},{8,10},{9,11},{10,... | collective-permute-start | bytes 110600 | tf_op jit(solution)/shard_map/ppermute | solution.py:481
  52.6 4.1 %collective-permute-start.2 = (f32[72,128]{1,0:T(8,128)S(1)}, f32[72,128]{1,0:T(8,128)S(1)}, u32[]{:S(2)}, u32[]{:S(2)}) collective-permute-start(f32[72,128]{1,0:T(8,128)S(1)} %get-tuple-element.19.own), channel_id=1, source_target_pairs={{0,3},{1,0},{2,1},{3,2},{4,7},{5,4},{6,5},{7,6},{8,11},{9,8},{10,9... | collective-permute-start | bytes 110600 | tf_op jit(solution)/shard_map/ppermute | solution.py:481
